TPU v7x, 32 devices: a whole 2x2x4 slice. The times are simulated.
32 devices in a mesh: groups: 2 (over x), gs: 8 (over z, y), sub: 2 (over core).
Axes of the slice: x: 2, y: 2, z: 4, core: 2. Of those that a mesh axis runs over, the one named last changes fastest.
Arguments:
- centres: float32 [3, 131072], P(None, ('groups', 'gs', 'sub')), parts along dimension 1, may hold values from -3 to 3
- log_scales: float32 [3, 131072], P(None, ('groups', 'gs', 'sub')), parts along dimension 1, may hold values from -3.7 to -1.4
- rotations: float32 [4, 131072], P(None, ('groups', 'gs', 'sub')), parts along dimension 1, may hold values from -1 to 2, as said below
- opacity_logits: float32 [131072], P(('groups', 'gs', 'sub')), parts along dimension 0, may hold values from -7 to -6.5
- colours: float32 [3, 131072], P(None, ('groups', 'gs', 'sub')), parts along dimension 1, may hold values from -6 to 6
- view_shift: float32 [8, 3], P('groups'), parts along dimension 0, may hold values from -0.2 to 0.2
- tile_ids: int32 [512], P(('groups', 'gs', 'sub')), parts along dimension 0, may hold values from 0 to 255, as said below
- tile_counts: int32 [512], P(('groups', 'gs', 'sub')), parts along dimension 0, may hold values from 256 to 512
- tile_lists: int32 [512, 512], P(('groups', 'gs', 'sub')), parts along dimension 0, may hold values from 0 to 4095, as said below
- send_index: int32 [32, 16, 256], P(('groups', 'gs', 'sub')), parts along dimension 0, may hold values from 0 to 16383, as said below
- image_cot: float32 [3, 131072], P(None, ('groups', 'gs', 'sub')), parts along dimension 1, may hold values from -6 to 6
Outputs:
- rendered: float32 [3, 131072], P(None, ('groups', 'gs', 'sub')), parts along dimension 1
- centre_grad: float32 [3, 131072], P(None, ('groups', 'gs', 'sub')), parts along dimension 1
- scale_grad: float32 [3, 131072], P(None, ('groups', 'gs', 'sub')), parts along dimension 1
- rotation_grad: float32 [4, 131072], P(None, ('groups', 'gs', 'sub')), parts along dimension 1
- opacity_grad: float32 [131072], P(('groups', 'gs', 'sub')), parts along dimension 0
- colour_grad: float32 [3, 131072], P(None, ('groups', 'gs', 'sub')), parts along dimension 1
There are 2 independent parts, one for each index of `groups`. A program takes and returns all parts, laid end to end along the dimension named above; each array names one. Nothing has to cross between parts.
Inputs may be any that keep to these rules, and one draw needn't show every extreme that they name: `send_index`: entries are view * 4096 + g; a Gaussian g of a source appears at most once among all its sends. `tile_ids`: A permutation of all tiles. `tile_lists`: slot numbers s * 256 + j of the owning device's received Gaussians; the live entries of one list are distinct, and every slot is named by some live entry of its device. `rotations`: first component 1 to 2, the others -1 to 1.
All inputs are finite; a program needn't handle non-finite values.
Results may differ from a plain program's by a relative error of at most 0.0003.
Values sent between devices are 32-bit elements; how exact they have to be, the bound alone decides.
No kernel may reach another device: no remote copies, remote signals or barrier semaphores. Data moves between devices by JAX's collectives and lax.ppermute only.
A program may use at most 64 MiB of HBM per device.

v0:
```python
from functools import partial

import jax
import jax.numpy as jnp
from jax import lax
from jax.sharding import PartitionSpec as P

VIEWS = 4
TILES_X = 32
LIST = 512
TILE_DEV = 16


FOCAL = 512.0
SH_ZERO = 0.28209479177387814
DILATION = 0.3
BACKGROUND = 1.0
DEPTH_OFFSET = 4.0


def project(centres, log_scales, rotations, opacity_logits, colours, view_shift, half_height):
    half_width = 8.0 * TILES_X
    camera_x = centres[0][None, :] + view_shift[:, 0:1]
    camera_y = centres[1][None, :] + view_shift[:, 1:2]
    camera_z = centres[2][None, :] + view_shift[:, 2:3] + DEPTH_OFFSET
    quat_norm = jnp.sqrt(jnp.sum(rotations * rotations, axis=0))
    quat_w = rotations[0] / quat_norm
    quat_x = rotations[1] / quat_norm
    quat_y = rotations[2] / quat_norm
    quat_z = rotations[3] / quat_norm
    rotation = [
        [
            1.0 - 2.0 * (quat_y * quat_y + quat_z * quat_z),
            2.0 * (quat_x * quat_y - quat_w * quat_z),
            2.0 * (quat_x * quat_z + quat_w * quat_y),
        ],
        [
            2.0 * (quat_x * quat_y + quat_w * quat_z),
            1.0 - 2.0 * (quat_x * quat_x + quat_z * quat_z),
            2.0 * (quat_y * quat_z - quat_w * quat_x),
        ],
        [
            2.0 * (quat_x * quat_z - quat_w * quat_y),
            2.0 * (quat_y * quat_z + quat_w * quat_x),
            1.0 - 2.0 * (quat_x * quat_x + quat_y * quat_y),
        ],
    ]
    scales = jnp.exp(log_scales)
    stretched = [
        [rotation[row_idx][col_idx] * scales[col_idx] for col_idx in range(3)]
        for row_idx in range(3)
    ]
    covariance = [
        [
            sum((stretched[row_idx][mid_idx] * stretched[col_idx][mid_idx] for mid_idx in range(3)))
            for col_idx in range(3)
        ]
        for row_idx in range(3)
    ]
    focal_z = FOCAL / camera_z
    shear_x = -FOCAL * camera_x / (camera_z * camera_z)
    shear_y = -FOCAL * camera_y / (camera_z * camera_z)
    screen_xx = (
        focal_z * focal_z * covariance[0][0]
        + 2.0 * focal_z * shear_x * covariance[0][2]
        + shear_x * shear_x * covariance[2][2]
        + DILATION
    )
    screen_yy = (
        focal_z * focal_z * covariance[1][1]
        + 2.0 * focal_z * shear_y * covariance[1][2]
        + shear_y * shear_y * covariance[2][2]
        + DILATION
    )
    screen_xy = (
        focal_z * focal_z * covariance[0][1]
        + focal_z * shear_y * covariance[0][2]
        + shear_x * focal_z * covariance[1][2]
        + shear_x * shear_y * covariance[2][2]
    )
    determinant = screen_xx * screen_yy - screen_xy * screen_xy
    mean_u = FOCAL * camera_x / camera_z + half_width
    mean_v = FOCAL * camera_y / camera_z + half_height
    opacity = jnp.broadcast_to(jax.nn.sigmoid(opacity_logits)[None, :], camera_z.shape)
    tints = [
        jnp.broadcast_to(0.5 + SH_ZERO * colours[channel][None, :], camera_z.shape)
        for channel in range(3)
    ]
    return jnp.stack(
        [
            mean_u,
            mean_v,
            screen_yy / determinant,
            -screen_xy / determinant,
            screen_xx / determinant,
            opacity,
        ]
        + tints
    )


def render_tile(params, tile_count, tile_id, tile_cot, tiles_view):
    local_id = tile_id % tiles_view
    anchor_x = (16 * (local_id % TILES_X)).astype(jnp.float32)
    anchor_y = (16 * (local_id // TILES_X)).astype(jnp.float32)
    within = jnp.arange(256, dtype=jnp.int32)
    pixel_x = anchor_x + (within % 16).astype(jnp.float32) + 0.5
    pixel_y = anchor_y + (within // 16).astype(jnp.float32) + 0.5
    is_live = jnp.arange(params.shape[1], dtype=jnp.int32) < tile_count

    def shade_tile(gathered):
        offset_x = pixel_x[:, None] - gathered[0][None, :]
        offset_y = pixel_y[:, None] - gathered[1][None, :]
        exponent = (
            -0.5
            * (
                gathered[2][None, :] * offset_x * offset_x
                + gathered[4][None, :] * offset_y * offset_y
            )
            - gathered[3][None, :] * offset_x * offset_y
        )
        coverage = jnp.where(is_live[None, :], gathered[5][None, :] * jnp.exp(exponent), 0.0)
        log_keep = jnp.log1p(-coverage)
        running = jnp.cumsum(log_keep, axis=1)
        weights = coverage * jnp.exp(running - log_keep)
        shaded = jnp.einsum("pl,cl->cp", weights, gathered[6:9], precision=lax.Precision.HIGHEST)
        return shaded + BACKGROUND * jnp.exp(running[:, -1])[None, :]

    shaded, pullback = jax.vjp(shade_tile, params)
    (params_grad,) = pullback(tile_cot)
    return (shaded, params_grad)


def shards(
    centres,
    log_scales,
    rotations,
    opacity_logits,
    colours,
    view_shift,
    tile_ids,
    tile_counts,
    tile_lists,
    send_index,
    image_cot,
):
    peer_count = lax.axis_size(("gs", "sub"))
    tiles_view = TILE_DEV * peer_count // VIEWS
    half_height = 8.0 * (tiles_view // TILES_X)

    def projector(centre_arg, scale_arg, rotation_arg, logit_arg, colour_arg):
        return project(
            centre_arg, scale_arg, rotation_arg, logit_arg, colour_arg, view_shift, half_height
        ).reshape(9, -1)

    projected, pull_raw = jax.vjp(
        projector, centres, log_scales, rotations, opacity_logits, colours
    )
    targets = send_index[0]
    capacity = targets.shape[1]
    outgoing = projected[:, targets]
    received = lax.all_to_all(outgoing, ("gs", "sub"), split_axis=1, concat_axis=1, tiled=True)
    received = received.reshape(9, peer_count * capacity)
    batches = TILE_DEV // 4
    gathered = jnp.moveaxis(received[:, tile_lists], 1, 0).reshape(batches, 4, 9, LIST)
    cot_tiles = jnp.moveaxis(image_cot.reshape(3, batches, 4, 256), 0, 2)
    shade_fn = jax.vmap(partial(render_tile, tiles_view=tiles_view))

    def render_batch(inputs):
        return shade_fn(inputs[0], inputs[1], inputs[2], inputs[3])

    shaded, tile_grads = lax.map(
        render_batch,
        (gathered, tile_counts.reshape(batches, 4), tile_ids.reshape(batches, 4), cot_tiles),
    )
    rendered = jnp.moveaxis(shaded, 2, 0).reshape(3, TILE_DEV * 256)
    flat_grads = jnp.moveaxis(tile_grads.reshape(TILE_DEV, 9, LIST), 1, 0).reshape(
        9, TILE_DEV * LIST
    )
    slot_grads = (
        jnp.zeros((9, peer_count * capacity), jnp.float32)
        .at[:, tile_lists.reshape(-1)]
        .add(flat_grads)
    )
    returned = lax.all_to_all(
        slot_grads.reshape(9, peer_count, capacity),
        ("gs", "sub"),
        split_axis=1,
        concat_axis=1,
        tiled=True,
    )
    proj_grad = (
        jnp.zeros(projected.shape, jnp.float32)
        .at[:, targets.reshape(-1)]
        .add(returned.reshape(9, peer_count * capacity))
    )
    raw_grads = pull_raw(proj_grad)
    return (rendered, raw_grads[0], raw_grads[1], raw_grads[2], raw_grads[3], raw_grads[4])


def solution(mesh):
    return jax.shard_map(
        shards,
        mesh=mesh,
        in_specs=(
            P(None, ("groups", "gs", "sub")),
            P(None, ("groups", "gs", "sub")),
            P(None, ("groups", "gs", "sub")),
            P(("groups", "gs", "sub")),
            P(None, ("groups", "gs", "sub")),
            P("groups", None),
            P(("groups", "gs", "sub")),
            P(("groups", "gs", "sub")),
            P(("groups", "gs", "sub"), None),
            P(("groups", "gs", "sub"), None, None),
            P(None, ("groups", "gs", "sub")),
        ),
        out_specs=(
            P(None, ("groups", "gs", "sub")),
            P(None, ("groups", "gs", "sub")),
            P(None, ("groups", "gs", "sub")),
            P(None, ("groups", "gs", "sub")),
            P(("groups", "gs", "sub")),
            P(None, ("groups", "gs", "sub")),
        ),
        check_vma=False,
    )
```

profile of v0, /device:TPU:0, one launch (start us, length us, event | category | flops | bytes accessed | tf_op | source)
XLA Modules:
  0.0 521.7 jit_solution(13571162419228397748)
XLA Ops:
  16.2 14.2 %gather_fusion = f32[4096,9]{1,0:T(8,128)S(1)} fusion(f32[9,16384]{0,1:T(8,128)} %copy.89, s32[4096]{0:T(1024)S(1)} %broadcast_clamp_fusion.1), kind=kCustom, calls=%fused_computation | custom fusion | bytes 311296 | tf_op jit(solution)/shard_map/gather | solution.py:161
  31.7 7.4 %all-to-all-start = ((f32[9,16,256]{2,0,1:T(8,128)}), f32[9,16,256]{2,0,1:T(8,128)S(1)}, u32[]{:S(2)}, u32[]{:S(2)}) async-start(f32[9,16,256]{2,0,1:T(8,128)} %bitcast.30), calls=%async_computation | async-start | bytes 524288 | tf_op jit(solution)/shard_map/all_to_all | solution.py:162
  41.8 7.4 %all-to-all-done = f32[9,16,256]{2,0,1:T(8,128)S(1)} async-done(((f32[9,16,256]{2,0,1:T(8,128)}), f32[9,16,256]{2,0,1:T(8,128)S(1)}, u32[]{:S(2)}, u32[]{:S(2)}) %all-to-all-start) | async-done | bytes 147488 | tf_op jit(solution)/shard_map/all_to_all | solution.py:162
  49.8 27.7 %gather_fusion.1 = f32[8192,9]{1,0:T(8,128)} fusion(f32[9,4096]{0,1:T(8,128)S(1)} %bitcast.225, s32[8192]{0:T(1024)S(1)} %broadcast_clamp_fusion), kind=kCustom, calls=%fused_computation.1 | custom fusion | bytes 622592 | tf_op jit(solution)/shard_map/gather | solution.py:165
  81.0 289.1 %while.15 = (s32[]{:T(128)}, f32[4,4,3,256]{3,2,1,0:T(4,128)}, f32[4,4,9,512]{3,2,1,0:T(8,128)}, f32[4,4,9,512]{3,2,1,0:T(8,128)}, s32[4,4]{1,0:T(4,128)}, /*ind...) while((s32[]{:T(128)}, f32[4,4,3,256]{3,2,1,0:T(4,128)}, ...), condition=%wide.region_13.14_spmd, body=%wide.region_1.13_spmd.sunk | while | flops 251810464 | bytes 67628912 | solution.py:172
  100.9 5.1 fusion.212
  115.0 5.4 %pad_add_fusion.4 = (f32[4,256,512]{2,1,0:T(8,128)}, f32[4,256,512]{2,1,0:T(8,128)}) fusion(f32[4,256,1]{2,1,0:T(8,128)S(1)} %get-tuple-element.382, f32[4,256,512]{2,1,0:T(8,128)S(1)} %reduce_window_sum.46, f32[4,512]{1,0:T(4,128)S(1)} %get-tuple-element.375, f32[4,512]{1,0:T(4,128)S(1)} %get-tuple-element.376, f32[4,256]{1,0:T(4,128)S(1)} %copy-done.12, ...), kind=kOutput, calls=%fused_computation.50.clone.1 | convolution fusion | flops 28311552 | bytes 6924292 | tf_op jit(solution)/shard_map/while/body/eval_jaxpr/vmap(transpose(jvp(pl,cl->cp)))/dot_general | solution.py:126
  127.4 10.2 %fusion.215 = f32[4,256,4,128]{1,2,3,0:T(4,128)S(1)} fusion(f32[4,256,4,128]{1,2,3,0:T(4,128)} %copy.155), kind=kOutput, calls=%fused_computation.403.clone.1 | output fusion | flops 66584576 | bytes 4194304 | tf_op jit(solution)/shard_map/reduce-window.18
  149.4 6.3 %fusion.216 = (f32[4,512]{1,0:T(4,128)S(1)}, f32[4,512]{1,0:T(4,128)S(1)}, f32[4,512]{1,0:T(4,128)S(1)}, f32[4,512]{1,0:T(4,128)S(1)}, f32[4,512]{1,0:T(4,128)S(1)}, /*index=5*/f32[4,512]{1,0:T(4,128)S(1)}) fusion(f32[4,512]{1,0:T(4,128)S(1)} %get-tuple-element.376, f32[4,256]{1,0:T(4,128)S(1)} %copy-done.12, f32[4,512]{1,0:T(4,128)S(1)} %get-tuple-element.378, ...), kind=kLoop, calls=%fused_computation.44.clone.1 | loop fusion | flops 27250688 | bytes 6400000 | tf_op jit(solution)/shard_map/while/body/eval_jaxpr/vmap(transpose(jvp()))/reduce_sum | solution.py:120
  169.4 5.1 fusion.212
  183.4 5.4 %pad_add_fusion.4 = (f32[4,256,512]{2,1,0:T(8,128)}, f32[4,256,512]{2,1,0:T(8,128)}) fusion(f32[4,256,1]{2,1,0:T(8,128)S(1)} %get-tuple-element.382, f32[4,256,512]{2,1,0:T(8,128)S(1)} %reduce_window_sum.46, f32[4,512]{1,0:T(4,128)S(1)} %get-tuple-element.375, f32[4,512]{1,0:T(4,128)S(1)} %get-tuple-element.376, f32[4,256]{1,0:T(4,128)S(1)} %copy-done.12, ...), kind=kOutput, calls=%fused_computation.50.clone.1 | convolution fusion | flops 28311552 | bytes 6924292 | tf_op jit(solution)/shard_map/while/body/eval_jaxpr/vmap(transpose(jvp(pl,cl->cp)))/dot_general | solution.py:126
  195.8 10.2 %fusion.215 = f32[4,256,4,128]{1,2,3,0:T(4,128)S(1)} fusion(f32[4,256,4,128]{1,2,3,0:T(4,128)} %copy.155), kind=kOutput, calls=%fused_computation.403.clone.1 | output fusion | flops 66584576 | bytes 4194304 | tf_op jit(solution)/shard_map/reduce-window.18
  217.9 6.3 %fusion.216 = (f32[4,512]{1,0:T(4,128)S(1)}, f32[4,512]{1,0:T(4,128)S(1)}, f32[4,512]{1,0:T(4,128)S(1)}, f32[4,512]{1,0:T(4,128)S(1)}, f32[4,512]{1,0:T(4,128)S(1)}, /*index=5*/f32[4,512]{1,0:T(4,128)S(1)}) fusion(f32[4,512]{1,0:T(4,128)S(1)} %get-tuple-element.376, f32[4,256]{1,0:T(4,128)S(1)} %copy-done.12, f32[4,512]{1,0:T(4,128)S(1)} %get-tuple-element.378, ...), kind=kLoop, calls=%fused_computation.44.clone.1 | loop fusion | flops 27250688 | bytes 6400000 | tf_op jit(solution)/shard_map/while/body/eval_jaxpr/vmap(transpose(jvp()))/reduce_sum | solution.py:120
  251.9 5.4 %pad_add_fusion.4 = (f32[4,256,512]{2,1,0:T(8,128)}, f32[4,256,512]{2,1,0:T(8,128)}) fusion(f32[4,256,1]{2,1,0:T(8,128)S(1)} %get-tuple-element.382, f32[4,256,512]{2,1,0:T(8,128)S(1)} %reduce_window_sum.46, f32[4,512]{1,0:T(4,128)S(1)} %get-tuple-element.375, f32[4,512]{1,0:T(4,128)S(1)} %get-tuple-element.376, f32[4,256]{1,0:T(4,128)S(1)} %copy-done.12, ...), kind=kOutput, calls=%fused_computation.50.clone.1 | convolution fusion | flops 28311552 | bytes 6924292 | tf_op jit(solution)/shard_map/while/body/eval_jaxpr/vmap(transpose(jvp(pl,cl->cp)))/dot_general | solution.py:126
  264.3 10.2 %fusion.215 = f32[4,256,4,128]{1,2,3,0:T(4,128)S(1)} fusion(f32[4,256,4,128]{1,2,3,0:T(4,128)} %copy.155), kind=kOutput, calls=%fused_computation.403.clone.1 | output fusion | flops 66584576 | bytes 4194304 | tf_op jit(solution)/shard_map/reduce-window.18
  286.3 6.3 %fusion.216 = (f32[4,512]{1,0:T(4,128)S(1)}, f32[4,512]{1,0:T(4,128)S(1)}, f32[4,512]{1,0:T(4,128)S(1)}, f32[4,512]{1,0:T(4,128)S(1)}, f32[4,512]{1,0:T(4,128)S(1)}, /*index=5*/f32[4,512]{1,0:T(4,128)S(1)}) fusion(f32[4,512]{1,0:T(4,128)S(1)} %get-tuple-element.376, f32[4,256]{1,0:T(4,128)S(1)} %copy-done.12, f32[4,512]{1,0:T(4,128)S(1)} %get-tuple-element.378, ...), kind=kLoop, calls=%fused_computation.44.clone.1 | loop fusion | flops 27250688 | bytes 6400000 | tf_op jit(solution)/shard_map/while/body/eval_jaxpr/vmap(transpose(jvp()))/reduce_sum | solution.py:120
  306.3 5.1 fusion.212
  320.3 5.4 %pad_add_fusion.4 = (f32[4,256,512]{2,1,0:T(8,128)}, f32[4,256,512]{2,1,0:T(8,128)}) fusion(f32[4,256,1]{2,1,0:T(8,128)S(1)} %get-tuple-element.382, f32[4,256,512]{2,1,0:T(8,128)S(1)} %reduce_window_sum.46, f32[4,512]{1,0:T(4,128)S(1)} %get-tuple-element.375, f32[4,512]{1,0:T(4,128)S(1)} %get-tuple-element.376, f32[4,256]{1,0:T(4,128)S(1)} %copy-done.12, ...), kind=kOutput, calls=%fused_computation.50.clone.1 | convolution fusion | flops 28311552 | bytes 6924292 | tf_op jit(solution)/shard_map/while/body/eval_jaxpr/vmap(transpose(jvp(pl,cl->cp)))/dot_general | solution.py:126
  332.8 10.2 %fusion.215 = f32[4,256,4,128]{1,2,3,0:T(4,128)S(1)} fusion(f32[4,256,4,128]{1,2,3,0:T(4,128)} %copy.155), kind=kOutput, calls=%fused_computation.403.clone.1 | output fusion | flops 66584576 | bytes 4194304 | tf_op jit(solution)/shard_map/reduce-window.18
  354.8 6.3 %fusion.216 = (f32[4,512]{1,0:T(4,128)S(1)}, f32[4,512]{1,0:T(4,128)S(1)}, f32[4,512]{1,0:T(4,128)S(1)}, f32[4,512]{1,0:T(4,128)S(1)}, f32[4,512]{1,0:T(4,128)S(1)}, /*index=5*/f32[4,512]{1,0:T(4,128)S(1)}) fusion(f32[4,512]{1,0:T(4,128)S(1)} %get-tuple-element.376, f32[4,256]{1,0:T(4,128)S(1)} %copy-done.12, f32[4,512]{1,0:T(4,128)S(1)} %get-tuple-element.378, ...), kind=kLoop, calls=%fused_computation.44.clone.1 | loop fusion | flops 27250688 | bytes 6400000 | tf_op jit(solution)/shard_map/while/body/eval_jaxpr/vmap(transpose(jvp()))/reduce_sum | solution.py:120
  373.7 44.8 %scatter_custom_fusion = f32[9,4096]{0,1:T(8,128)S(1)} fusion(s32[8192]{0:T(1024)} %bitcast.329, f32[8192,9]{1,0:T(8,128)} %bitcast.228, f32[]{:T(128)} %constant.193.clone.1), kind=kCustom, calls=%fused_computation.141 | custom fusion | flops 73728 | bytes 147968 | tf_op jit(solution)/shard_map/scatter-add | solution.py:183
  423.4 10.0 %all-to-all-done.1 = f32[9,16,256]{2,0,1:T(8,128)S(1)} async-done(((f32[9,16,256]{2,0,1:T(8,128)}), f32[9,16,256]{2,0,1:T(8,128)S(1)}, u32[]{:S(2)}, u32[]{:S(2)}) %all-to-all-start.1) | async-done | bytes 147488 | tf_op jit(solution)/shard_map/all_to_all | solution.py:185
  434.3 26.1 %scatter_custom_fusion.1 = f32[9,16384]{0,1:T(8,128)} fusion(s32[4096]{0:T(1024)S(1)} %bitcast.330, f32[4096,9]{1,0:T(8,128)S(1)} %copy.97, f32[]{:T(128)} %constant.193.clone.1), kind=kCustom, calls=%fused_computation.139 | custom fusion | flops 36864 | bytes 589828 | tf_op jit(solution)/shard_map/scatter-add | solution.py:195
  460.4 50.7 %slice_reduce_fusion.2 = (f32[16384]{0:T(1024)S(1)}, f32[16384]{0:T(1024)S(1)}, f32[16384]{0:T(1024)S(1)}, f32[16384]{0:T(1024)S(1)}, f32[16384]{0:T(1024)S(1)},...) fusion(f32[9,16384]{0,1:T(8,128)} %scatter_custom_fusion.1), kind=kLoop, calls=%fused_computation.132 | loop fusion | bytes 1179648 | tf_op jit(solution)/shard_map/transpose(jvp())/unstack | solution.py:89
  (585 shorter events, 211.6 us)
Async XLA Ops:
  0.6 6.8 %copy-start.87 = (f32[3,4096]{1,0:T(4,128)S(1)}, f32[3,4096]{1,0:T(4,128)}, u32[]{:S(2)}) copy-start(f32[3,4096]{1,0:T(4,128)} %param.13) | copy-start | bytes 147460
  0.7 8.1 %copy-start.88 = (f32[3,4096]{1,0:T(4,128)S(1)}, f32[3,4096]{1,0:T(4,128)}, u32[]{:S(2)}) copy-start(f32[3,4096]{1,0:T(4,128)} %param.17) | copy-start | bytes 147460
  1.6 7.5 %copy-start.9 = (f32[3,4096]{1,0:T(4,128)}, f32[3,4096]{1,0:T(4,128)S(1)}, u32[]{:S(2)}) copy-start(f32[3,4096]{1,0:T(4,128)S(1)} %exp.46) | copy-start | bytes 147460
  16.2 22.9 %copy-start.65 = (s32[16,512]{1,0:T(8,128)S(1)}, s32[16,512]{1,0:T(8,128)}, u32[]{:S(2)}) copy-start(s32[16,512]{1,0:T(8,128)} %param.21) | copy-start | bytes 98308
  16.2 23.6 %copy-start.93 = (s32[16]{0:T(128)S(1)}, s32[16]{0:T(128)}, u32[]{:S(2)}) copy-start(s32[16]{0:T(128)} %param.20) | copy-start | bytes 196
  16.2 24.3 %copy-start.94 = (s32[16]{0:T(128)S(1)}, s32[16]{0:T(128)}, u32[]{:S(2)}) copy-start(s32[16]{0:T(128)} %param.19) | copy-start | bytes 196
  31.7 17.4 %all-to-all-start = ((f32[9,16,256]{2,0,1:T(8,128)}), f32[9,16,256]{2,0,1:T(8,128)S(1)}, u32[]{:S(2)}, u32[]{:S(2)}) async-start(f32[9,16,256]{2,0,1:T(8,128)} %bitcast.30), calls=%async_computation | async-start | bytes 524288 | tf_op jit(solution)/shard_map/all_to_all | solution.py:162
  373.7 49.7 %copy-start.78 = (s32[1,1,16,256]{3,1,2,0:T(1,128)S(1)}, s32[1,1,16,256]{3,1,2,0:T(1,128)}, u32[]{:S(2)}) copy-start(s32[1,1,16,256]{3,1,2,0:T(1,128)} %copy.122) | copy-start | bytes 49156
  419.8 13.5 %all-to-all-start.1 = ((f32[9,16,256]{2,0,1:T(8,128)}), f32[9,16,256]{2,0,1:T(8,128)S(1)}, u32[]{:S(2)}, u32[]{:S(2)}) async-start(f32[9,16,256]{2,0,1:T(8,128)} %copy.95), calls=%async_computation.1 | async-start | bytes 524288 | tf_op jit(solution)/shard_map/all_to_all | solution.py:185
  460.4 51.6 %copy-start.76 = (f32[4096]{0:T(1024)S(1)}, f32[4096]{0:T(1024)}, u32[]{:S(2)}) copy-start(f32[4096]{0:T(1024)} %param.16) | copy-start | bytes 49156
  460.4 52.3 %copy-start.17 = (f32[1,4096]{1,0:T(1,128)S(1)}, f32[1,4096]{1,0:T(1,128)}, u32[]{:S(2)}) copy-start(f32[1,4096]{1,0:T(1,128)} %copy-done.16) | copy-start | bytes 49156
  460.4 52.3 %copy-start.19 = (f32[1,4096]{1,0:T(1,128)S(1)}, f32[1,4096]{1,0:T(1,128)}, u32[]{:S(2)}) copy-start(f32[1,4096]{1,0:T(1,128)} %copy-done.18) | copy-start | bytes 49156
  460.4 52.3 %copy-start.21 = (f32[1,4096]{1,0:T(1,128)S(1)}, f32[1,4096]{1,0:T(1,128)}, u32[]{:S(2)}) copy-start(f32[1,4096]{1,0:T(1,128)} %copy-done.20) | copy-start | bytes 49156
  460.4 52.3 %copy-start.23 = (f32[1,4096]{1,0:T(1,128)S(1)}, f32[1,4096]{1,0:T(1,128)}, u32[]{:S(2)}) copy-start(f32[1,4096]{1,0:T(1,128)} %copy-done.22) | copy-start | bytes 49156
  460.4 52.3 %copy-start.25 = (f32[1,4096]{1,0:T(1,128)S(1)}, f32[1,4096]{1,0:T(1,128)}, u32[]{:S(2)}) copy-start(f32[1,4096]{1,0:T(1,128)} %copy-done.24) | copy-start | bytes 49156
  460.4 52.3 %copy-start.27 = (f32[1,4096]{1,0:T(1,128)S(1)}, f32[1,4096]{1,0:T(1,128)}, u32[]{:S(2)}) copy-start(f32[1,4096]{1,0:T(1,128)} %copy-done.26) | copy-start | bytes 49156
  460.4 52.3 %copy-start.29 = (f32[1,4096]{1,0:T(1,128)S(1)}, f32[1,4096]{1,0:T(1,128)}, u32[]{:S(2)}) copy-start(f32[1,4096]{1,0:T(1,128)} %copy-done.28) | copy-start | bytes 49156
  460.4 52.3 %copy-start.33 = (f32[1,4096]{1,0:T(1,128)S(1)}, f32[1,4096]{1,0:T(1,128)}, u32[]{:S(2)}) copy-start(f32[1,4096]{1,0:T(1,128)} %copy-done.32) | copy-start | bytes 49156
  460.4 52.3 %copy-start.50 = (f32[1,4096]{1,0:T(1,128)S(1)}, f32[1,4096]{1,0:T(1,128)}, u32[]{:S(2)}) copy-start(f32[1,4096]{1,0:T(1,128)} %copy-done.49) | copy-start | bytes 49156
  511.5 6.6 %copy-start.80 = (f32[1,4096]{1,0:T(1,128)S(1)}, f32[1,4096]{1,0:T(1,128)}, u32[]{:S(2)}) copy-start(f32[1,4096]{1,0:T(1,128)} %get-tuple-element.232) | copy-start | bytes 49156
  511.6 6.6 %copy-start.68 = (f32[1,4096]{1,0:T(1,128)S(1)}, f32[1,4096]{1,0:T(1,128)}, u32[]{:S(2)}) copy-start(f32[1,4096]{1,0:T(1,128)} %get-tuple-element.219) | copy-start | bytes 49156
  511.7 6.6 %copy-start.67 = (f32[1,4096]{1,0:T(1,128)S(1)}, f32[1,4096]{1,0:T(1,128)}, u32[]{:S(2)}) copy-start(f32[1,4096]{1,0:T(1,128)} %get-tuple-element.217) | copy-start | bytes 49156
  512.0 8.0 %copy-start.15 = (f32[4,4096]{1,0:T(4,128)S(1)}, f32[4,4096]{1,0:T(4,128)}, u32[]{:S(2)}) copy-start(f32[4,4096]{1,0:T(4,128)} %param.15) | copy-start | bytes 196612
  512.7 8.1 %copy-start.42 = (f32[3,4096]{1,0:T(4,128)S(1)}, f32[3,4096]{1,0:T(4,128)}, u32[]{:S(2)}) copy-start(f32[3,4096]{1,0:T(4,128)} %param.14) | copy-start | bytes 147460
  (121 other events, 323.2 us)
where the time goes:
time: 529 us; the launch traced here: 522 us
  local copies, waits for them, and re-layouts  220 us (42%)
  other arithmetic  201 us (38%)
  matrix products  52.8 us (10%)
  waiting for transfers between devices  17.3 us (3%)
  loops' own time  16.8 us (3%)
  starting transfers between devices  10.9 us (2%)
    another operation x40, local copies, waits for them, and re-layouts  82.1 us
    another operation x24, other arithmetic  81.3 us
    another operation x12, local copies, waits for them, and re-layouts, project(): jnp.stack([mean_u, mean_v, screen_yy / determinant, -screen_xy / determin...  56.6 us
    dot_general x12, matrix products, shade_tile(): jnp.einsum('pl,cl->cp', weights, gathered[6:9], precision=lax.Precision.H...  52.8 us
    scatter-add x1, other arithmetic, shards(): slot_grads = jnp.zeros((9, peer_count * capacity), jnp.float32).at[:, til...  44.8 us
    gather x1, local copies, waits for them, and re-layouts, shards(): received[:, tile_lists]  27.7 us
    scatter-add x1, other arithmetic, shards(): proj_grad = jnp.zeros(projected.shape, jnp.float32).at[:, targets.reshape...  26.1 us
    reduce_sum x4, other arithmetic, shade_tile(): gathered[3][None, :] * offset_x * offset_y  25.2 us
  transfers between devices with their start and end apart: 2, of which 2 were waited for; matrix products, arithmetic and copies ran while one was open for 1% of the time, Pallas kernels for 0%

commit v1 on v0

v1 whole, which is shorter than its diff:
```python
import math

import jax
import jax.numpy as jnp
from jax import lax
from jax.experimental import pallas as pl
from jax.experimental.pallas import tpu as pltpu
from jax.sharding import PartitionSpec as P

TILES_X = 32
FOCAL = 512.0
SH_ZERO = 0.28209479177387814
DILATION = 0.3
BACKGROUND = 1.0
DEPTH_OFFSET = 4.0
LOG2E = math.log2(math.e)
PARAMS = 9
ROW = PARAMS * 128
AXES = ("groups", "gs", "sub")
PEERS = ("gs", "sub")

BF16 = jnp.bfloat16
F32 = jnp.float32
NN = (((1,), (0,)), ((), ()))
NT = (((1,), (1,)), ((), ()))
TN = (((0,), (0,)), ((), ()))


def dot(lhs, rhs, dims=NN):
    return lax.dot_general(lhs, rhs, dims, preferred_element_type=F32)


def iota(shape, dim):
    return lax.broadcasted_iota(jnp.int32, shape, dim)


def halves(value):
    high = value.astype(BF16)
    return high, (value - high.astype(F32)).astype(BF16)


def lookup(row_of, low, high, rows):
    found = [jnp.zeros(low[0].shape, F32) for _ in low]
    for row in range(rows):
        spread = jnp.broadcast_to(row_of(row), low[0].shape)
        for pos in range(len(low)):
            taken = jnp.take_along_axis(spread, low[pos], axis=1, mode="promise_in_bounds")
            found[pos] = jnp.where(high[pos] == row, taken, found[pos])
    return found


def project(raw, shift):
    centres, log_scales, rotations, logit, colours, half_height = raw
    half_width = 8.0 * TILES_X
    camera_x = centres[0] + shift[0]
    camera_y = centres[1] + shift[1]
    camera_z = centres[2] + shift[2] + DEPTH_OFFSET
    inv_norm = 1.0 / jnp.sqrt(sum(part * part for part in rotations))
    quat_w, quat_x, quat_y, quat_z = [part * inv_norm for part in rotations]
    rotation = [
        [
            1.0 - 2.0 * (quat_y * quat_y + quat_z * quat_z),
            2.0 * (quat_x * quat_y - quat_w * quat_z),
            2.0 * (quat_x * quat_z + quat_w * quat_y),
        ],
        [
            2.0 * (quat_x * quat_y + quat_w * quat_z),
            1.0 - 2.0 * (quat_x * quat_x + quat_z * quat_z),
            2.0 * (quat_y * quat_z - quat_w * quat_x),
        ],
        [
            2.0 * (quat_x * quat_z - quat_w * quat_y),
            2.0 * (quat_y * quat_z + quat_w * quat_x),
            1.0 - 2.0 * (quat_x * quat_x + quat_y * quat_y),
        ],
    ]
    scales = [jnp.exp(part) for part in log_scales]
    stretched = [[rotation[i][j] * scales[j] for j in range(3)] for i in range(3)]

    def covariance(i, j):
        return sum(stretched[i][mid] * stretched[j][mid] for mid in range(3))

    cov_xx, cov_xy, cov_xz = covariance(0, 0), covariance(0, 1), covariance(0, 2)
    cov_yy, cov_yz, cov_zz = covariance(1, 1), covariance(1, 2), covariance(2, 2)
    inv_z = 1.0 / camera_z
    focal_z = FOCAL * inv_z
    ratio_x = camera_x * inv_z
    ratio_y = camera_y * inv_z
    shear_x = -focal_z * ratio_x
    shear_y = -focal_z * ratio_y
    screen_xx = (
        focal_z * focal_z * cov_xx
        + 2.0 * focal_z * shear_x * cov_xz
        + shear_x * shear_x * cov_zz
        + DILATION
    )
    screen_yy = (
        focal_z * focal_z * cov_yy
        + 2.0 * focal_z * shear_y * cov_yz
        + shear_y * shear_y * cov_zz
        + DILATION
    )
    screen_xy = (
        focal_z * focal_z * cov_xy
        + focal_z * shear_y * cov_xz
        + shear_x * focal_z * cov_yz
        + shear_x * shear_y * cov_zz
    )
    inv_det = 1.0 / (screen_xx * screen_yy - screen_xy * screen_xy)
    return [
        FOCAL * ratio_x + half_width,
        FOCAL * ratio_y + half_height,
        screen_yy * inv_det,
        -screen_xy * inv_det,
        screen_xx * inv_det,
        1.0 / (1.0 + jnp.exp(-logit)),
    ] + [0.5 + SH_ZERO * part for part in colours]


def load_dense(ref, scratch, first, rows):
    count = ref.shape[0]
    for row in range(rows):
        scratch[pl.ds(first + row, count, stride=rows), :] = ref[:, row * 128 : row * 128 + 128]


def view_shifts(view, shift_ref):
    chosen = []
    for axis in range(3):
        value = jnp.full(view.shape, shift_ref[0, axis], F32)
        for other in range(1, shift_ref.shape[0]):
            value = jnp.where(view == other, shift_ref[other, axis], value)
        chosen.append(value)
    return chosen


def raw_rows(scratch, logit_ref, rows, chunk):
    def part(index):
        return scratch[index * rows + chunk * 8 : index * rows + chunk * 8 + 8, :]

    return (
        [part(i) for i in range(3)],
        [part(i) for i in range(3, 6)],
        [part(i) for i in range(6, 10)],
        logit_ref[chunk * 8 : chunk * 8 + 8, :],
        [part(i) for i in range(10, 13)],
    )


def load_raw(refs, scratch, rows):
    first = 0
    for ref in refs:
        load_dense(ref, scratch, first, rows)
        first += ref.shape[0] * rows


def pre_kernel(
    half_height,
    shift_ref,
    centre_ref,
    scale_ref,
    rotation_ref,
    logit_ref,
    colour_ref,
    send_ref,
    out_ref,
    inverse_ref,
    view_ref,
    raw,
    index,
    table,
):
    rows = logit_ref.shape[0]
    owned = rows * 128
    load_raw((centre_ref, scale_ref, rotation_ref, colour_ref), raw, rows)
    per = send_ref.shape[1] // 128
    peers = send_ref.shape[0]
    for part in range(per):
        index[pl.ds(part, peers, stride=per), :] = send_ref[:, part * 128 : part * 128 + 128]
    total = jnp.zeros((2 * rows, 128), F32)
    group = 8
    for start in range(0, rows, group):
        lefts, rights = [], []
        for row in range(start, start + group):
            entry = index[row : row + 1, :]
            local = entry % owned
            slot = row * 128 + iota((1, 128), 1)
            first = (slot >> 6).astype(F32)
            second = ((slot & 63) + 64 * (entry // owned)).astype(F32)
            match = jnp.broadcast_to(local >> 7, (rows, 128)) == iota((rows, 128), 0)
            lefts.append(
                jnp.concatenate([jnp.where(match, first, 0.0), jnp.where(match, second, 0.0)], 0)
            )
            rights.append(
                jnp.where(
                    jnp.broadcast_to(local & 127, (128, 128)) == iota((128, 128), 0), 1.0, 0.0
                )
            )
        left = jnp.concatenate(lefts, 1).astype(BF16)
        right = jnp.concatenate(rights, 1).astype(BF16)
        total = total + dot(left, right, NT)
    whole = (total + 0.5).astype(jnp.int32)
    second = whole[rows:]
    inverse_ref[...] = whole[:rows] * 64 + (second & 63)
    view_ref[...] = second >> 6
    for chunk in range(rows // 8):
        parts = raw_rows(raw, logit_ref, rows, chunk)
        shift = view_shifts(view_ref[chunk * 8 : chunk * 8 + 8, :], shift_ref)
        for c, value in enumerate(project(parts + (half_height,), shift)):
            table[c * rows + chunk * 8 : c * rows + chunk * 8 + 8, :] = value
    local = [index[i * 8 : i * 8 + 8, :] % owned for i in range(rows // 8)]
    low = [value & 127 for value in local]
    high = [value >> 7 for value in local]

    def gather(c, carry):
        found = lookup(lambda row: table[pl.ds(c * rows + row, 1), :], low, high, rows)
        lane = pl.multiple_of(c * 128, 128)
        for i in range(rows // 8):
            for s in range(8):
                out_ref[i * 8 + s, :, pl.ds(lane, 128)] = found[i][s : s + 1, :]
        return carry

    lax.fori_loop(0, PARAMS, gather, 0)


def render_kernel(
    tiles_view,
    count_ref,
    id_ref,
    table_ref,
    list_ref,
    cot_ref,
    image_ref,
    grad_ref,
    gathered,
    coefs,
    moments,
    grads,
    exclusive,
    inclusive,
    partial_ref,
    beta_ref,
    slot_ref,
    slots,
):
    tiles, length = list_ref.shape
    blocks = length // 128
    rows = table_ref.shape[0]
    vregs = [(8 * i, 128 * b) for i in range(tiles // 8) for b in range(blocks)]
    stride = 16 * blocks

    def dense(ref, first, lane):
        return ref[first : first + 8, lane : lane + 128]

    def spot(first, lane, k):
        return pl.ds((first * blocks + lane // 128) * 16 + k, 8, stride=stride)

    index = [dense(list_ref, *pos) for pos in vregs]
    low = [value & 127 for value in index]
    high = [value >> 7 for value in index]

    def gather(c, carry):
        offset = pl.multiple_of(c * 128, 128)
        found = lookup(lambda row: table_ref[row, :, pl.ds(offset, 128)], low, high, rows)
        for (first, lane), value in zip(vregs, found):
            gathered[c, first : first + 8, lane : lane + 128] = value
        return carry

    lax.fori_loop(0, PARAMS, gather, 0)
    for (first, lane), value in zip(vregs, index):
        slots[pl.ds(first * blocks + lane // 128, 8, stride=blocks), :] = value

    sublane = iota((8, 128), 0)
    mid_x, mid_y, live = [], [], []
    for i in range(tiles // 8):
        x = jnp.zeros((8, 128), jnp.int32)
        y = x
        n = x
        for s in range(8):
            local = lax.rem(id_ref[i * 8 + s], tiles_view)
            x = jnp.where(sublane == s, 16 * lax.rem(local, TILES_X) + 8, x)
            y = jnp.where(sublane == s, 16 * lax.div(local, TILES_X) + 8, y)
            n = jnp.where(sublane == s, count_ref[i * 8 + s], n)
        mid_x.append(x.astype(F32))
        mid_y.append(y.astype(F32))
        live.append(n)

    def entry(first, lane):
        u, w, a, b, e, o = [gathered[c, first : first + 8, lane : lane + 128] for c in range(6)]
        return u - mid_x[first // 8], w - mid_y[first // 8], a, b, e, o

    coefs[...] = jnp.zeros(coefs.shape, F32)
    for first, lane in vregs:
        du, dw, a, b, e, o = entry(first, lane)
        is_live = iota((8, 128), 1) + lane < live[first // 8]
        slope_x = a * du + b * dw
        slope_y = e * dw + b * du
        level = -0.5 * (du * slope_x + dw * slope_y) + jnp.log(o)
        values = [-0.5 * a, -0.5 * e, -b, slope_x, slope_y, level]
        for k, value in enumerate(values):
            dead = -1000.0 if k == 5 else 0.0
            coefs[spot(first, lane, k), :] = jnp.where(is_live, value * LOG2E, dead)
        for k in range(3):
            tint = gathered[6 + k, first : first + 8, lane : lane + 128]
            coefs[spot(first, lane, 8 + k), :] = tint - BACKGROUND

    before = iota((256, 256), 0) & 127
    after = iota((256, 256), 1)
    is_sum = after >= 128
    exclusive[...] = jnp.where(is_sum | (before < after), 1.0, 0.0).astype(BF16)
    inclusive[...] = jnp.where(is_sum | (before <= after), 1.0, 0.0).astype(BF16)
    feature = iota((8, 256), 0)
    pixel = iota((8, 256), 1)
    px = (pixel & 15).astype(F32) - 7.5
    py = (pixel >> 4).astype(F32) - 7.5
    features = jnp.where(feature == 0, px * px, 0.0)
    for k, value in enumerate([py * py, px * py, px, py, jnp.ones_like(px)]):
        features = jnp.where(feature == k + 1, value, features)
    no_rows = jnp.zeros((8, 256), F32)
    moment_rows = jnp.concatenate([features, no_rows], 0).astype(BF16)
    blank = jnp.zeros((24, 128), F32)

    def render(t, carry):
        lanes = pl.ds(pl.multiple_of(t * 256, 256), 256)
        cot = jnp.concatenate([cot_ref[:, lanes], jnp.zeros((5, 256), F32)], 0)
        cot_high = cot.astype(BF16).astype(F32)
        cot_low = cot - cot_high
        left = jnp.concatenate(
            [features, features, features, cot_high, cot_high, cot_low], 0
        ).astype(BF16)
        left = left.T
        cot_rows = jnp.concatenate([cot_high, cot_low], 0).astype(BF16)
        run = None
        run_grad = None
        image = jnp.zeros((16, 256), F32)
        for b in range(blocks):
            base = pl.multiple_of((t * blocks + b) * 16, 16)
            coef = coefs[pl.ds(base, 8), :]
            tint = coefs[pl.ds(base + 8, 8), :]
            coef_high = coef.astype(BF16).astype(F32)
            rest = coef - coef_high
            coef_mid = rest.astype(BF16).astype(F32)
            coef_low = rest - coef_mid
            tint_high = tint.astype(BF16).astype(F32)
            tint_low = tint - tint_high
            shape_rows = jnp.concatenate([coef_high, coef_mid, coef_low], 0)
            tint_rows = jnp.concatenate([tint_high, tint_low, tint_high], 0)
            right = jnp.concatenate(
                [
                    jnp.concatenate([shape_rows, blank], 1),
                    jnp.concatenate([blank, tint_rows], 1),
                ],
                0,
            ).astype(BF16)
            both = dot(left, right)
            alpha = jnp.exp2(both[:, :128])
            shade = both[:, 128:]
            keep = alpha * (-LOG2E + alpha * (-LOG2E / 2.0 + alpha * (-LOG2E / 3.0)))
            sums = dot(jnp.concatenate(halves(keep), 1), exclusive[...])
            logs = sums[:, :128]
            if b == 0:
                run = sums[:, 128:]
            else:
                logs = logs + run
                run = run + sums[:, 128:]
            weight = alpha * jnp.exp2(logs)
            share = weight * shade
            weights = jnp.concatenate(halves(weight), 1)
            tints = jnp.concatenate([tint_high, tint_low], 0).astype(BF16)
            image = image + dot(jnp.concatenate([tints, tints], 1), weights, NT)
            tint_grad = dot(cot_rows, weights)
            tint_grad = tint_grad[:8] + tint_grad[8:]
            moments[pl.ds(base + 8, 8), :] = tint_grad[:, :128] + tint_grad[:, 128:]
            sums = dot(jnp.concatenate(halves(share), 1), inclusive[...])
            prefix = sums[:, :128]
            if b == 0:
                run_grad = sums[:, 128:]
            else:
                prefix = prefix + run_grad
                run_grad = run_grad + sums[:, 128:]
            beta = alpha * (1.0 + alpha * (1.0 + alpha))
            beta_ref[:, b * 128 : b * 128 + 128] = beta
            partial_ref[:, b * 128 : b * 128 + 128] = share + prefix * beta
        image_ref[:, lanes] = BACKGROUND + (image[:8] + image[8:])[:3]
        for b in range(blocks):
            base = pl.multiple_of((t * blocks + b) * 16, 16)
            here = slice(b * 128, b * 128 + 128)
            slope = partial_ref[:, here] - run_grad * beta_ref[:, here]
            summed = dot(moment_rows, jnp.concatenate(halves(slope), 1))
            moments[pl.ds(base, 8), :] = summed[:8, :128] + summed[:8, 128:]
        return carry

    lax.fori_loop(0, tiles, render, 0)

    for first, lane in vregs:
        du, dw, a, b, e, o = entry(first, lane)
        m_xx, m_yy, m_xy, m_x, m_y, m_one = [moments[spot(first, lane, k), :] for k in range(6)]
        d_x = m_x - du * m_one
        d_y = m_y - dw * m_one
        values = [
            a * d_x + b * d_y,
            e * d_y + b * d_x,
            -0.5 * (m_xx - du * (m_x + d_x)),
            -(m_xy - dw * m_x - du * d_y),
            -0.5 * (m_yy - dw * (m_y + d_y)),
            m_one / o,
        ] + [moments[spot(first, lane, 8 + k), :] for k in range(3)]
        for k, value in enumerate(values):
            grads[spot(first, lane, k), :] = value

    slot_ref[...] = jnp.zeros(slot_ref.shape, F32)

    def scatter(t, carry):
        lefts, rights = [], []
        for b in range(blocks):
            base = pl.multiple_of((t * blocks + b) * 16, 16)
            entry_slot = slots[pl.ds(t * blocks + b, 1), :]
            match = jnp.broadcast_to(entry_slot >> 7, (rows, 128)) == iota((rows, 128), 0)
            where = jnp.broadcast_to(entry_slot & 127, (128, 128)) == iota((128, 128), 0)
            right = jnp.where(where, 1.0, 0.0).astype(BF16)
            high_rows, low_rows = [], []
            for c in range(PARAMS):
                value = grads[pl.ds(base + c, 1), :]
                value_high = value.astype(BF16).astype(F32)
                high_rows.append(jnp.where(match, value_high, 0.0))
                low_rows.append(jnp.where(match, value - value_high, 0.0))
            lefts.append(jnp.concatenate(high_rows, 0).astype(BF16))
            lefts.append(jnp.concatenate(low_rows, 0).astype(BF16))
            rights += [right, right]
        slot_ref[...] += dot(jnp.concatenate(lefts, 1), jnp.concatenate(rights, 1), NT)
        return carry

    lax.fori_loop(0, tiles, scatter, 0)

    for c in range(PARAMS):
        for row in range(rows):
            grad_ref[row, :, c * 128 : c * 128 + 128] = slot_ref[
                c * rows + row : c * rows + row + 1, :
            ]


def post_kernel(
    half_height,
    shift_ref,
    centre_ref,
    scale_ref,
    rotation_ref,
    logit_ref,
    colour_ref,
    inverse_ref,
    view_ref,
    table_ref,
    centre_out,
    scale_out,
    rotation_out,
    logit_out,
    colour_out,
    raw,
    grads,
    dense_out,
):
    rows = logit_ref.shape[0]
    load_raw((centre_ref, scale_ref, rotation_ref, colour_ref), raw, rows)
    index = [inverse_ref[i * 8 : i * 8 + 8, :] for i in range(rows // 8)]
    low = [value & 127 for value in index]
    high = [value >> 7 for value in index]

    def gather(c, carry):
        offset = pl.multiple_of(c * 128, 128)
        found = lookup(lambda row: table_ref[row, :, pl.ds(offset, 128)], low, high, rows)
        for i in range(rows // 8):
            grads[c, i * 8 : i * 8 + 8, :] = found[i]
        return carry

    lax.fori_loop(0, PARAMS, gather, 0)
    for chunk in range(rows // 8):
        parts = raw_rows(raw, logit_ref, rows, chunk)
        shift = view_shifts(view_ref[chunk * 8 : chunk * 8 + 8, :], shift_ref)
        _, pull = jax.vjp(lambda *args: project(args + (half_height,), shift), *parts)
        back = pull([grads[c, chunk * 8 : chunk * 8 + 8, :] for c in range(PARAMS)])
        flat = back[0] + back[1] + back[2] + back[4]
        for k, value in enumerate(flat):
            dense_out[k * rows + chunk * 8 : k * rows + chunk * 8 + 8, :] = value
        logit_out[chunk * 8 : chunk * 8 + 8, :] = back[3]
    first = 0
    for ref in (centre_out, scale_out, rotation_out, colour_out):
        count = ref.shape[0]
        for row in range(rows):
            ref[:, row * 128 : row * 128 + 128] = dense_out[
                pl.ds(first + row, count, stride=rows), :
            ]
        first += count * rows


def exchange(table, peers, capacity):
    if capacity % 128 == 0:
        return lax.all_to_all(table, PEERS, split_axis=0, concat_axis=0, tiled=True)
    rows = table.shape[0]
    per = 128 // capacity
    chunks = table.reshape(rows, PARAMS, per, capacity).transpose(0, 2, 1, 3)
    chunks = chunks.reshape(peers, 1, PARAMS * capacity)
    moved = lax.all_to_all(chunks, PEERS, split_axis=0, concat_axis=0, tiled=True)
    moved = moved.reshape(rows, per, PARAMS, capacity).transpose(0, 2, 1, 3)
    return moved.reshape(rows, 1, ROW)


VMEM = pl.BlockSpec(memory_space=pltpu.VMEM)
SMEM = pl.BlockSpec(memory_space=pltpu.SMEM)
LIMIT = pltpu.CompilerParams(vmem_limit_bytes=40 * 1024 * 1024)


def shards(
    centres,
    log_scales,
    rotations,
    opacity_logits,
    colours,
    view_shift,
    tile_ids,
    tile_counts,
    tile_lists,
    send_index,
    image_cot,
):
    owned = centres.shape[1]
    rows = owned // 128
    peers, capacity = send_index.shape[1:]
    tiles, length = tile_lists.shape
    views = view_shift.shape[0]
    tiles_view = tiles * peers // views
    half_height = 8.0 * (tiles_view // TILES_X)
    assert peers * capacity == owned
    logits = opacity_logits.reshape(rows, 128)
    targets = send_index[0] if capacity % 128 == 0 else send_index.reshape(rows, 128)
    outgoing, inverse, view = pl.pallas_call(
        lambda *refs: pre_kernel(half_height, *refs),
        out_shape=(
            jax.ShapeDtypeStruct((rows, 1, ROW), F32),
            jax.ShapeDtypeStruct((rows, 128), jnp.int32),
            jax.ShapeDtypeStruct((rows, 128), jnp.int32),
        ),
        in_specs=[SMEM] + [VMEM] * 6,
        out_specs=(VMEM,) * 3,
        scratch_shapes=[
            pltpu.VMEM((13 * rows, 128), F32),
            pltpu.VMEM((rows, 128), jnp.int32),
            pltpu.VMEM((PARAMS * rows, 128), F32),
        ],
        compiler_params=LIMIT,
        name="project_and_pack",
    )(view_shift, centres, log_scales, rotations, logits, colours, targets)
    received = exchange(outgoing, peers, capacity)
    rendered, slot_grads = pl.pallas_call(
        lambda *refs: render_kernel(tiles_view, *refs),
        out_shape=(
            jax.ShapeDtypeStruct((3, tiles * 256), F32),
            jax.ShapeDtypeStruct((rows, 1, ROW), F32),
        ),
        in_specs=[SMEM] * 2 + [VMEM] * 3,
        out_specs=(VMEM,) * 2,
        scratch_shapes=[
            pltpu.VMEM((PARAMS, tiles, length), F32),
            pltpu.VMEM((tiles * length // 8, 128), F32),
            pltpu.VMEM((tiles * length // 8, 128), F32),
            pltpu.VMEM((tiles * length // 8, 128), F32),
            pltpu.VMEM((256, 256), BF16),
            pltpu.VMEM((256, 256), BF16),
            pltpu.VMEM((256, length), F32),
            pltpu.VMEM((256, length), F32),
            pltpu.VMEM((PARAMS * rows, 128), F32),
            pltpu.VMEM((tiles * length // 128, 128), jnp.int32),
        ],
        compiler_params=LIMIT,
        name="render",
    )(tile_counts, tile_ids, received, tile_lists, image_cot)
    returned = exchange(slot_grads, peers, capacity)
    shapes = [jax.ShapeDtypeStruct((n, owned), F32) for n in (3, 3, 4, 3)]
    shapes.insert(3, jax.ShapeDtypeStruct((rows, 128), F32))
    grads = pl.pallas_call(
        lambda *refs: post_kernel(half_height, *refs),
        out_shape=tuple(shapes),
        in_specs=[SMEM] + [VMEM] * 8,
        out_specs=(VMEM,) * 5,
        scratch_shapes=[
            pltpu.VMEM((13 * rows, 128), F32),
            pltpu.VMEM((PARAMS, rows, 128), F32),
            pltpu.VMEM((13 * rows, 128), F32),
        ],
        compiler_params=LIMIT,
        name="unpack_and_project_back",
    )(
        view_shift, centres, log_scales, rotations, logits, colours, inverse, view, returned
    )
    return (rendered, grads[0], grads[1], grads[2], grads[3].reshape(owned), grads[4])


def solution(mesh):
    wide = P(None, AXES)
    flat = P(AXES)
    return jax.shard_map(
        shards,
        mesh=mesh,
        in_specs=(
            wide,
            wide,
            wide,
            flat,
            wide,
            P("groups", None),
            flat,
            flat,
            P(AXES, None),
            P(AXES, None, None),
            wide,
        ),
        out_specs=(wide, wide, wide, wide, flat, wide),
        check_vma=False,
    )
```

time: 529 us -> 88 us (0.17); the launches traced: 522 us -> 87.4 us
  local copies, waits for them, and re-layouts: 220 us -> 5.51 us
  other arithmetic: 201 us -> 0 us
  Pallas kernels: 0 us -> 54.7 us
  matrix products: 52.8 us -> 0 us
  blocking collectives: 0 us -> 26.4 us
  waiting for transfers between devices: 17.3 us -> 0 us
  loops' own time: 16.8 us -> 0 us
  starting transfers between devices: 10.9 us -> 0 us
    another operation x52 -> x0, local copies, waits for them, and re-layouts: 139 us -> none
    another operation x24 -> x0, other arithmetic: 81.3 us -> none
    scatter-add x2 -> x0, other arithmetic: 70.9 us -> none  [the longest x1 44.8 us: shards(): slot_grads = jnp.zeros((9, peer_count * capacity), jnp.float32).at[:, til...]
    pallas_call x0 -> x3, Pallas kernels: none -> 54.7 us  [the longest x1 44.1 us: shards(): pl.pallas_call(lambda *refs: render_kernel(tiles_view, *refs), out_shape=...]
    dot_general x12 -> x0, matrix products: 52.8 us -> none  [shade_tile(): jnp.einsum('pl,cl->cp', weights, gathered[6:9], precision=lax.Precision.H...]
    gather x3 -> x0, local copies, waits for them, and re-layouts: 43.2 us -> none  [the longest x1 27.7 us: shards(): received[:, tile_lists]]
    reduce_sum x14 -> x0, other arithmetic: 28.1 us -> none  [the longest x4 25.2 us: shade_tile(): gathered[3][None, :] * offset_x * offset_y]
    all_to_all x0 -> x2, blocking collectives: none -> 26.4 us  [exchange(): return lax.all_to_all(table, PEERS, split_axis=0, concat_axis=0, tiled=True)]
  transfers between devices with their start and end apart: 2 -> 0, of which waited for: 2 -> 0; matrix products, arithmetic and copies ran while one was open for 1% -> 0% of each run, Pallas kernels for 0% -> 0%
where the time goes in v1:
time: 88 us; the launch traced here: 87.4 us
  Pallas kernels  54.7 us (62%)
  blocking collectives  26.4 us (30%)
  local copies, waits for them, and re-layouts  5.51 us (6%)
    pallas_call x1, Pallas kernels, shards(): pl.pallas_call(lambda *refs: render_kernel(tiles_view, *refs), out_shape=...  44.1 us
    all_to_all x2, blocking collectives, exchange(): return lax.all_to_all(table, PEERS, split_axis=0, concat_axis=0, tiled=True)  26.4 us
    unnamed x32, local copies, waits for them, and re-layouts  5.51 us
    pallas_call x1, Pallas kernels, shards(): pl.pallas_call(lambda *refs: post_kernel(half_height, *refs), out_shape=t...  5.49 us
    pallas_call x1, Pallas kernels, shards(): pl.pallas_call(lambda *refs: pre_kernel(half_height, *refs), out_shape=(j...  5.13 us

profile of v1, /device:TPU:0, one launch (start us, length us, event | category | flops | bytes accessed | tf_op | source)
XLA Modules:
  0.0 87.4 jit_solution(11992184462460987023)
XLA Ops:
  0.6 0.0 copy-start.13
  0.6 0.7 copy-done.13
  1.3 0.8 copy-done
  2.2 0.8 copy-done.2
  3.0 0.8 copy-done.4
  3.8 0.8 copy-done.6
  4.7 0.7 copy-done.8
  5.4 0.7 copy-done.12
  6.1 5.1 %project_and_pack.1 = (f32[32,1,1152]{2,1,0:T(1,128)S(1)}, s32[32,128]{1,0:T(8,128)S(1)}, s32[32,128]{1,0:T(8,128)S(1)}) custom-call(f32[4,3]{1,0:T(4,128)S(1)} %copy-done.13, f32[3,4096]{1,0:T(4,128)S(1)} %copy-done, f32[3,4096]{1,0:T(4,128)S(1)} %copy-done.2, f32[4,4096]{1,0:T(4,128)S(1)} %copy-done.4, f32[32,128]{1,0:T(8,128)S(1)} %bitcast.3, ...), custom_call_target="tpu_custom_call" | custom-call | tf_op jit(solution)/shard_map/project_and_pack/pallas_call | solution.py:534
  11.2 0.0 copy-start.10
  11.3 0.0 copy-start.11
  11.3 0.0 copy-start.14
  11.3 0.0 copy-start.15
  11.3 15.5 %all_to_all.10.refs_2_ = f32[32,1,1152]{2,1,0:T(1,128)S(1)} all-to-all(f32[32,1,1152]{2,1,0:T(1,128)S(1)} %get-tuple-element.16), channel_id=1, replica_groups=mesh['groups'=2,'gs'=8,'sub'=2] {'gs','sub'}, dimensions={0} | all-to-all | bytes 294912 | tf_op jit(solution)/shard_map/all_to_all | solution.py:496
  26.8 0.0 copy-done.10
  26.8 0.0 copy-done.11
  26.8 0.0 copy-done.14
  26.8 0.0 copy-done.15
  26.8 44.1 %render.1 = (f32[3,4096]{1,0:T(4,128)}, f32[32,1,1152]{2,1,0:T(1,128)S(1)}) custom-call(s32[16]{0:T(128)S(1)} %copy-done.14, s32[16]{0:T(128)S(1)} %copy-done.15, f32[32,1,1152]{2,1,0:T(1,128)S(1)} %all_to_all.10.refs_2_, s32[16,512]{1,0:T(8,128)S(1)} %copy-done.11, f32[3,4096]{1,0:T(4,128)S(1)} %copy-done.10), custom_call_target="tpu_custom_call" | custom-call | tf_op jit(solution)/shard_map/render/pallas_call | solution.py:552
  71.0 0.0 copy-start.9
  71.0 10.9 %all_to_all.11.refs_8_ = f32[32,1,1152]{2,1,0:T(1,128)S(1)} all-to-all(f32[32,1,1152]{2,1,0:T(1,128)S(1)} %get-tuple-element.20), channel_id=1, replica_groups=mesh['groups'=2,'gs'=8,'sub'=2] {'gs','sub'}, dimensions={0} | all-to-all | bytes 294912 | tf_op jit(solution)/shard_map/all_to_all | solution.py:496
  81.9 0.0 copy-done.1
  81.9 0.0 copy-done.5
  81.9 5.5 %unpack_and_project_back.1 = (f32[3,4096]{1,0:T(4,128)}, f32[3,4096]{1,0:T(4,128)}, f32[4,4096]{1,0:T(4,128)}, f32[32,128]{1,0:T(8,128)}, f32[3,4096]{1,0:T(4,128)}) custom-call(f32[4,3]{1,0:T(4,128)S(1)} %copy-done.13, f32[3,4096]{1,0:T(4,128)S(1)} %copy-done.1, f32[3,4096]{1,0:T(4,128)S(1)} %copy-done.3, f32[4,4096]{1,0:T(4,128)S(1)} %copy-done.5, ...), custom_call_target="tpu_custom_call" | custom-call | tf_op jit(solution)/shard_map/unpack_and_project_back/pallas_call | solution.py:578
  (13 shorter events, 0.0 us)
Async XLA Ops:
  0.6 0.7 copy-start.13
  1.3 0.8 copy-start
  2.2 0.8 copy-start.2
  3.0 0.8 copy-start.4
  3.8 0.8 copy-start.6
  4.7 0.7 copy-start.8
  5.4 0.7 copy-start.12
  11.2 15.6 %copy-start.10 = (f32[3,4096]{1,0:T(4,128)S(1)}, f32[3,4096]{1,0:T(4,128)}, u32[]{:S(2)}) copy-start(f32[3,4096]{1,0:T(4,128)} %refs_4_.1) | copy-start | bytes 147460
  11.3 15.6 %copy-start.11 = (s32[16,512]{1,0:T(8,128)S(1)}, s32[16,512]{1,0:T(8,128)}, u32[]{:S(2)}) copy-start(s32[16,512]{1,0:T(8,128)} %refs_3_.4) | copy-start | bytes 98308
  11.3 15.5 %copy-start.14 = (s32[16]{0:T(128)S(1)}, s32[16]{0:T(128)}, u32[]{:S(2)}) copy-start(s32[16]{0:T(128)} %refs_0_.4) | copy-start | bytes 196
  11.3 15.5 %copy-start.15 = (s32[16]{0:T(128)S(1)}, s32[16]{0:T(128)}, u32[]{:S(2)}) copy-start(s32[16]{0:T(128)} %refs_1_.4) | copy-start | bytes 196
  71.0 10.9 %copy-start.1 = (f32[3,4096]{1,0:T(4,128)S(1)}, f32[3,4096]{1,0:T(4,128)}, u32[]{:S(2)}) copy-start(f32[3,4096]{1,0:T(4,128)} %refs_1_.5) | copy-start | bytes 147460
  71.0 10.9 %copy-start.3 = (f32[3,4096]{1,0:T(4,128)S(1)}, f32[3,4096]{1,0:T(4,128)}, u32[]{:S(2)}) copy-start(f32[3,4096]{1,0:T(4,128)} %refs_2_.3) | copy-start | bytes 147460
  71.0 10.9 %copy-start.5 = (f32[4,4096]{1,0:T(4,128)S(1)}, f32[4,4096]{1,0:T(4,128)}, u32[]{:S(2)}) copy-start(f32[4,4096]{1,0:T(4,128)} %refs_3_.5) | copy-start | bytes 196612
  71.0 11.0 %copy-start.7 = (f32[3,4096]{1,0:T(4,128)S(1)}, f32[3,4096]{1,0:T(4,128)}, u32[]{:S(2)}) copy-start(f32[3,4096]{1,0:T(4,128)} %refs_5_.3) | copy-start | bytes 147460
  71.0 11.0 %copy-start.9 = (f32[4096]{0:T(1024)S(1)}, f32[4096]{0:T(1024)}, u32[]{:S(2)}) copy-start(f32[4096]{0:T(1024)} %param.14) | copy-start | bytes 49156

commit v2 on v1

v2 whole, which is shorter than its diff:
```python
import math

import jax
import jax.numpy as jnp
from jax import lax
from jax.experimental import pallas as pl
from jax.experimental.pallas import tpu as pltpu
from jax.sharding import PartitionSpec as P

TILES_X = 32
FOCAL = 512.0
SH_ZERO = 0.28209479177387814
DILATION = 0.3
BACKGROUND = 1.0
DEPTH_OFFSET = 4.0
LOG2E = math.log2(math.e)
PARAMS = 9
ROW = PARAMS * 128
AXES = ("groups", "gs", "sub")
PEERS = ("gs", "sub")

BF16 = jnp.bfloat16
F32 = jnp.float32
NN = (((1,), (0,)), ((), ()))
NT = (((1,), (1,)), ((), ()))
TN = (((0,), (0,)), ((), ()))


def dot(lhs, rhs, dims=NN):
    return lax.dot_general(lhs, rhs, dims, preferred_element_type=F32)


def iota(shape, dim):
    return lax.broadcasted_iota(jnp.int32, shape, dim)


def halves(value):
    high = value.astype(BF16)
    return high, (value - high.astype(F32)).astype(BF16)


def lookup(row_of, index, rows):
    low = index & 127
    high = index >> 7
    found = jnp.zeros(index.shape, F32)
    for row in range(rows):
        spread = jnp.broadcast_to(row_of(row), index.shape)
        taken = jnp.take_along_axis(spread, low, axis=1, mode="promise_in_bounds")
        found = jnp.where(high == row, taken, found)
    return found


def project(raw, shift):
    centres, log_scales, rotations, logit, colours, half_height = raw
    half_width = 8.0 * TILES_X
    camera_x = centres[0] + shift[0]
    camera_y = centres[1] + shift[1]
    camera_z = centres[2] + shift[2] + DEPTH_OFFSET
    inv_norm = 1.0 / jnp.sqrt(sum(part * part for part in rotations))
    quat_w, quat_x, quat_y, quat_z = [part * inv_norm for part in rotations]
    rotation = [
        [
            1.0 - 2.0 * (quat_y * quat_y + quat_z * quat_z),
            2.0 * (quat_x * quat_y - quat_w * quat_z),
            2.0 * (quat_x * quat_z + quat_w * quat_y),
        ],
        [
            2.0 * (quat_x * quat_y + quat_w * quat_z),
            1.0 - 2.0 * (quat_x * quat_x + quat_z * quat_z),
            2.0 * (quat_y * quat_z - quat_w * quat_x),
        ],
        [
            2.0 * (quat_x * quat_z - quat_w * quat_y),
            2.0 * (quat_y * quat_z + quat_w * quat_x),
            1.0 - 2.0 * (quat_x * quat_x + quat_y * quat_y),
        ],
    ]
    scales = [jnp.exp(part) for part in log_scales]
    stretched = [[rotation[i][j] * scales[j] for j in range(3)] for i in range(3)]

    def covariance(i, j):
        return sum(stretched[i][mid] * stretched[j][mid] for mid in range(3))

    cov_xx, cov_xy, cov_xz = covariance(0, 0), covariance(0, 1), covariance(0, 2)
    cov_yy, cov_yz, cov_zz = covariance(1, 1), covariance(1, 2), covariance(2, 2)
    inv_z = 1.0 / camera_z
    focal_z = FOCAL * inv_z
    ratio_x = camera_x * inv_z
    ratio_y = camera_y * inv_z
    shear_x = -focal_z * ratio_x
    shear_y = -focal_z * ratio_y
    screen_xx = (
        focal_z * focal_z * cov_xx
        + 2.0 * focal_z * shear_x * cov_xz
        + shear_x * shear_x * cov_zz
        + DILATION
    )
    screen_yy = (
        focal_z * focal_z * cov_yy
        + 2.0 * focal_z * shear_y * cov_yz
        + shear_y * shear_y * cov_zz
        + DILATION
    )
    screen_xy = (
        focal_z * focal_z * cov_xy
        + focal_z * shear_y * cov_xz
        + shear_x * focal_z * cov_yz
        + shear_x * shear_y * cov_zz
    )
    inv_det = 1.0 / (screen_xx * screen_yy - screen_xy * screen_xy)
    return [
        FOCAL * ratio_x + half_width,
        FOCAL * ratio_y + half_height,
        screen_yy * inv_det,
        -screen_xy * inv_det,
        screen_xx * inv_det,
        1.0 / (1.0 + jnp.exp(-logit)),
    ] + [0.5 + SH_ZERO * part for part in colours]


def load_dense(ref, dense, first, rows):
    count = ref.shape[0]
    for row in range(rows):
        dense[pl.ds(first + row, count, stride=rows), :] = ref[:, row * 128 : row * 128 + 128]


def view_shifts(view, shift_ref):
    chosen = []
    for axis in range(3):
        value = jnp.full(view.shape, shift_ref[0, axis], F32)
        for other in range(1, shift_ref.shape[0]):
            value = jnp.where(view == other, shift_ref[other, axis], value)
        chosen.append(value)
    return chosen


def raw_rows(raw, rows, chunk):
    parts = [raw[i * rows + chunk * 8 : i * rows + chunk * 8 + 8, :] for i in range(14)]
    return parts[:3], parts[3:6], parts[6:10], parts[13], parts[10:13]


def pre_kernel(
    half_height,
    shift_ref,
    centre_hbm,
    scale_hbm,
    rotation_hbm,
    logit_hbm,
    colour_hbm,
    send_hbm,
    list_hbm,
    cot_hbm,
    out_ref,
    inverse_ref,
    view_ref,
    raw,
    slots,
    cot_ref,
    centre_ref,
    scale_ref,
    rotation_ref,
    colour_ref,
    send_ref,
    list_ref,
    index,
    table,
    arrived,
):
    rows = table.shape[0] // PARAMS
    owned = rows * 128
    logit_ref = raw.at[pl.ds(13 * rows, rows), :]
    pairs = [
        (send_hbm, send_ref),
        (centre_hbm, centre_ref),
        (scale_hbm, scale_ref),
        (rotation_hbm, rotation_ref),
        (colour_hbm, colour_ref),
        (logit_hbm, logit_ref),
        (list_hbm, list_ref),
        (cot_hbm, cot_ref),
    ]
    copies = [
        pltpu.make_async_copy(source, target, arrived.at[i])
        for i, (source, target) in enumerate(pairs)
    ]
    for copy in copies:
        copy.start()
    copies[0].wait()
    per = send_ref.shape[1] // 128
    peers = send_ref.shape[0]
    for part in range(per):
        index[pl.ds(part, peers, stride=per), :] = send_ref[:, part * 128 : part * 128 + 128]
    total = jnp.zeros((2 * rows, 128), F32)
    group = 8
    for start in range(0, rows, group):
        lefts, rights = [], []
        for row in range(start, start + group):
            entry = index[row : row + 1, :]
            local = entry % owned
            slot = row * 128 + iota((1, 128), 1)
            first = (slot >> 6).astype(F32)
            second = ((slot & 63) + 64 * (entry // owned)).astype(F32)
            match = jnp.broadcast_to(local >> 7, (rows, 128)) == iota((rows, 128), 0)
            lefts.append(
                jnp.concatenate([jnp.where(match, first, 0.0), jnp.where(match, second, 0.0)], 0)
            )
            rights.append(
                jnp.where(
                    jnp.broadcast_to(local & 127, (128, 128)) == iota((128, 128), 0), 1.0, 0.0
                )
            )
        left = jnp.concatenate(lefts, 1).astype(BF16)
        right = jnp.concatenate(rights, 1).astype(BF16)
        total = total + dot(left, right, NT)
    whole = (total + 0.5).astype(jnp.int32)
    second = whole[rows:]
    inverse_ref[...] = whole[:rows] * 64 + (second & 63)
    view_ref[...] = second >> 6
    for copy in copies[1:6]:
        copy.wait()
    first = 0
    for ref in (centre_ref, scale_ref, rotation_ref, colour_ref):
        load_dense(ref, raw, first, rows)
        first += ref.shape[0] * rows
    for chunk in range(rows // 8):
        parts = raw_rows(raw, rows, chunk)
        shift = view_shifts(view_ref[chunk * 8 : chunk * 8 + 8, :], shift_ref)
        for c, value in enumerate(project(parts + (half_height,), shift)):
            table[c * rows + chunk * 8 : c * rows + chunk * 8 + 8, :] = value
    local = [index[i * 8 : i * 8 + 8, :] % owned for i in range(rows // 8)]

    def gather(c, carry):
        lane = pl.multiple_of(c * 128, 128)
        for i in range(rows // 8):
            found = lookup(lambda row: table[pl.ds(c * rows + row, 1), :], local[i], rows)
            for s in range(8):
                out_ref[i * 8 + s, :, pl.ds(lane, 128)] = found[s : s + 1, :]
        return carry

    lax.fori_loop(0, PARAMS, gather, 0)
    copies[6].wait()
    tiles, length = list_ref.shape
    blocks = length // 128
    lane = iota((8, 128), 1)
    for b in range(blocks):
        entry = run_entry(lane, b, length)
        for i in range(tiles // 8):
            moved = jnp.zeros((8, 128), jnp.int32)
            for source in range(blocks):
                value = list_ref[i * 8 : i * 8 + 8, source * 128 : source * 128 + 128]
                taken = jnp.take_along_axis(
                    value, entry & 127, axis=1, mode="promise_in_bounds"
                )
                moved = jnp.where(entry >> 7 == source, taken, moved)
            slots[pl.ds(i * 8 * blocks + b, 8, stride=blocks), :] = moved
    copies[7].wait()


def run_entry(lane, block, length):
    return (lane & 7) * (length // 8) + block * 16 + (lane >> 3)


def render_kernel(
    tiles_view,
    length,
    count_ref,
    id_ref,
    table_ref,
    slots,
    cot_ref,
    image_ref,
    grad_ref,
    gathered,
    coefs,
    moments,
    grads,
    slot_ref,
    *buffers,
):
    blocks = length // 128
    tiles = slots.shape[0] // blocks
    rows = table_ref.shape[0]
    places = [(8 * i, b) for i in range(tiles // 8) for b in range(blocks)]
    stride = 16 * blocks

    def spot(first, b, k):
        return pl.ds((first * blocks + b) * 16 + k, 8, stride=stride)

    index = [slots[pl.ds(first * blocks + b, 8, stride=blocks), :] for first, b in places]

    def gather(c, carry):
        offset = pl.multiple_of(c * 128, 128)
        for pos, value in enumerate(index):
            gathered[c, pos] = lookup(
                lambda row: table_ref[row, :, pl.ds(offset, 128)], value, rows
            )
        return carry

    lax.fori_loop(0, PARAMS, gather, 0)

    sublane = iota((8, 128), 0)
    lane = iota((8, 128), 1)
    mid_x, mid_y, live = [], [], []
    for i in range(tiles // 8):
        x = jnp.zeros((8, 128), jnp.int32)
        y = x
        n = x
        for s in range(8):
            local = lax.rem(id_ref[i * 8 + s], tiles_view)
            x = jnp.where(sublane == s, 16 * lax.rem(local, TILES_X) + 8, x)
            y = jnp.where(sublane == s, 16 * lax.div(local, TILES_X) + 8, y)
            n = jnp.where(sublane == s, count_ref[i * 8 + s], n)
        mid_x.append(x.astype(F32))
        mid_y.append(y.astype(F32))
        live.append(n)

    def entry(pos):
        u, w, a, b, e, o = [gathered[c, pos] for c in range(6)]
        first = places[pos][0]
        return u - mid_x[first // 8], w - mid_y[first // 8], a, b, e, o

    coefs[...] = jnp.zeros(coefs.shape, F32)
    for pos, (first, block) in enumerate(places):
        du, dw, a, b, e, o = entry(pos)
        is_live = run_entry(lane, block, length) < live[first // 8]
        slope_x = a * du + b * dw
        slope_y = e * dw + b * du
        level = -0.5 * (du * slope_x + dw * slope_y) + jnp.log(o)
        values = [-0.5 * a, -0.5 * e, -b, slope_x, slope_y, level]
        for k, value in enumerate(values):
            dead = -1000.0 if k == 5 else 0.0
            coefs[spot(first, block, k), :] = jnp.where(is_live, value * LOG2E, dead)
        for k in range(3):
            coefs[spot(first, block, 8 + k), :] = gathered[6 + k, pos] - BACKGROUND

    feature = iota((8, 256), 0)
    pixel = iota((8, 256), 1)
    px = (pixel & 15).astype(F32) - 7.5
    py = (pixel >> 4).astype(F32) - 7.5
    features = jnp.where(feature == 0, px * px, 0.0)
    for k, value in enumerate([py * py, px * py, px, py, jnp.ones_like(px)]):
        features = jnp.where(feature == k + 1, value, features)
    blank = jnp.zeros((24, 256), F32)
    moment_rows = jnp.concatenate([features, jnp.zeros((8, 256), F32)], 0)
    moment_rows = jnp.concatenate([moment_rows, moment_rows], 1).astype(BF16)
    run_row = iota((8, 256), 0)

    def earlier_product(value):
        for step in (1, 2, 4):
            moved = pltpu.roll(value, step, 0)
            value = value * jnp.where(run_row >= step, moved, 1.0)
        return jnp.where(run_row >= 1, pltpu.roll(value, 1, 0), 1.0)

    def later_sum(value):
        for step in (1, 2, 4):
            moved = pltpu.roll(value, 8 - step, 0)
            value = value + jnp.where(run_row < 8 - step, moved, 0.0)
        return jnp.where(run_row < 7, pltpu.roll(value, 7, 0), 0.0)

    def render(t, alpha_ref, share_ref, weights, slopes):
        lanes = pl.ds(pl.multiple_of(t * 256, 256), 256)
        cot = jnp.concatenate([cot_ref[:, lanes], jnp.zeros((5, 256), F32)], 0)
        cot_high = cot.astype(BF16).astype(F32)
        cot_low = cot - cot_high
        right = jnp.concatenate(
            [
                jnp.concatenate([features, features, features, blank], 0),
                jnp.concatenate([blank, cot_high, cot_high, cot_low], 0),
            ],
            1,
        ).astype(BF16)
        cot_rows = jnp.concatenate([cot_high, cot_low], 0)
        cot_rows = jnp.concatenate([cot_rows, cot_rows], 1).astype(BF16)
        lefts, tints = [], []
        for b in range(blocks):
            base = pl.multiple_of((t * blocks + b) * 16, 16)
            coef = coefs[pl.ds(base, 8), :]
            tint = coefs[pl.ds(base + 8, 8), :]
            coef_high = coef.astype(BF16).astype(F32)
            rest = coef - coef_high
            coef_mid = rest.astype(BF16).astype(F32)
            tint_high = tint.astype(BF16).astype(F32)
            tint_low = tint - tint_high
            lefts.append(
                jnp.concatenate(
                    [coef_high, coef_mid, rest - coef_mid, tint_high, tint_low, tint_high], 0
                )
            )
            tints.append(jnp.concatenate([tint_high, tint_low], 0))
        left = jnp.concatenate(lefts, 1).astype(BF16)
        tint_rows = jnp.concatenate(tints, 1).astype(BF16)
        both = dot(left, right, TN)
        steps = length // 16
        left_over = jnp.ones((8, 256), F32)
        for step in range(steps):
            here = slice(step * 16, step * 16 + 16)
            alpha = jnp.exp2(both[here, :256])
            alpha_ref[here, :] = alpha
            keep = 1.0 - alpha
            left_over = left_over * (keep[:8] * keep[8:])
        through = earlier_product(left_over)
        total = jnp.zeros((8, 256), F32)
        for step in range(steps):
            here = slice(step * 16, step * 16 + 16)
            alpha = alpha_ref[here, :]
            first = alpha[:8] * through
            through = through - first
            second = alpha[8:] * through
            through = through - second
            weight = jnp.concatenate([first, second], 0)
            high, low = halves(weight)
            weights[here, :256] = high
            weights[here, 256:] = low
            share = weight * both[here, 256:]
            share_ref[here, :] = share
            total = total + (share[:8] + share[8:])
        image = dot(tint_rows, weights[:, :256])
        image_ref[:, lanes] = BACKGROUND + (image[:8] + image[8:])[:3]
        tint_grad = dot(cot_rows, weights[...], NT)
        tint_grad = tint_grad[:8] + tint_grad[8:]
        behind = later_sum(total)
        for step in reversed(range(steps)):
            here = slice(step * 16, step * 16 + 16)
            alpha = alpha_ref[here, :]
            share = share_ref[here, :]
            beta = alpha * (1.0 + alpha * (1.0 + alpha))
            second = share[8:] - beta[8:] * behind
            behind = behind + share[8:]
            first = share[:8] - beta[:8] * behind
            behind = behind + share[:8]
            high, low = halves(jnp.concatenate([first, second], 0))
            slopes[here, :256] = high
            slopes[here, 256:] = low
        summed = dot(moment_rows, slopes[...], NT)
        for b in range(blocks):
            base = pl.multiple_of((t * blocks + b) * 16, 16)
            here = slice(b * 128, b * 128 + 128)
            moments[pl.ds(base, 8), :] = summed[:8, here]
            moments[pl.ds(base + 8, 8), :] = tint_grad[:, here]

    def pair(t, carry):
        render(2 * t, *buffers[:4])
        render(2 * t + 1, *buffers[4:])
        return carry

    lax.fori_loop(0, tiles // 2, pair, 0)

    for pos, (first, block) in enumerate(places):
        du, dw, a, b, e, o = entry(pos)
        m_xx, m_yy, m_xy, m_x, m_y, m_one = [moments[spot(first, block, k), :] for k in range(6)]
        d_x = m_x - du * m_one
        d_y = m_y - dw * m_one
        values = [
            a * d_x + b * d_y,
            e * d_y + b * d_x,
            -0.5 * (m_xx - du * (m_x + d_x)),
            -(m_xy - dw * m_x - du * d_y),
            -0.5 * (m_yy - dw * (m_y + d_y)),
            m_one / o,
        ] + [moments[spot(first, block, 8 + k), :] for k in range(3)]
        for k, value in enumerate(values):
            grads[spot(first, block, k), :] = value

    slot_ref[...] = jnp.zeros(slot_ref.shape, F32)

    def scatter(t, carry):
        lefts, rights = [], []
        for b in range(blocks):
            base = pl.multiple_of((t * blocks + b) * 16, 16)
            entry_slot = slots[pl.ds(t * blocks + b, 1), :]
            match = jnp.broadcast_to(entry_slot >> 7, (rows, 128)) == iota((rows, 128), 0)
            where = jnp.broadcast_to(entry_slot & 127, (128, 128)) == iota((128, 128), 0)
            right = jnp.where(where, 1.0, 0.0).astype(BF16)
            high_rows, low_rows = [], []
            for c in range(PARAMS):
                value = grads[pl.ds(base + c, 1), :]
                value_high = value.astype(BF16).astype(F32)
                high_rows.append(jnp.where(match, value_high, 0.0))
                low_rows.append(jnp.where(match, value - value_high, 0.0))
            lefts.append(jnp.concatenate(high_rows, 0).astype(BF16))
            lefts.append(jnp.concatenate(low_rows, 0).astype(BF16))
            rights += [right, right]
        slot_ref[...] += dot(jnp.concatenate(lefts, 1), jnp.concatenate(rights, 1), NT)
        return carry

    lax.fori_loop(0, tiles, scatter, 0)

    for c in range(PARAMS):
        for row in range(rows):
            grad_ref[row, :, c * 128 : c * 128 + 128] = slot_ref[
                c * rows + row : c * rows + row + 1, :
            ]


def post_kernel(
    half_height,
    shift_ref,
    raw,
    inverse_ref,
    view_ref,
    table_ref,
    centre_out,
    scale_out,
    rotation_out,
    logit_out,
    colour_out,
    grads,
    dense_out,
):
    rows = logit_out.shape[0]
    index = [inverse_ref[i * 8 : i * 8 + 8, :] for i in range(rows // 8)]

    def gather(c, carry):
        offset = pl.multiple_of(c * 128, 128)
        for i in range(rows // 8):
            grads[c, i * 8 : i * 8 + 8, :] = lookup(
                lambda row: table_ref[row, :, pl.ds(offset, 128)], index[i], rows
            )
        return carry

    lax.fori_loop(0, PARAMS, gather, 0)
    for chunk in range(rows // 8):
        parts = raw_rows(raw, rows, chunk)
        shift = view_shifts(view_ref[chunk * 8 : chunk * 8 + 8, :], shift_ref)
        _, pull = jax.vjp(lambda *args: project(args + (half_height,), shift), *parts)
        back = pull([grads[c, chunk * 8 : chunk * 8 + 8, :] for c in range(PARAMS)])
        flat = back[0] + back[1] + back[2] + back[4]
        for k, value in enumerate(flat):
            dense_out[k * rows + chunk * 8 : k * rows + chunk * 8 + 8, :] = value
        logit_out[chunk * 8 : chunk * 8 + 8, :] = back[3]
    first = 0
    for ref in (centre_out, scale_out, rotation_out, colour_out):
        count = ref.shape[0]
        for row in range(rows):
            ref[:, row * 128 : row * 128 + 128] = dense_out[
                pl.ds(first + row, count, stride=rows), :
            ]
        first += count * rows


def exchange(table, peers, capacity):
    if capacity % 128 == 0:
        return lax.all_to_all(table, PEERS, split_axis=0, concat_axis=0, tiled=True)
    rows = table.shape[0]
    per = 128 // capacity
    chunks = table.reshape(rows, PARAMS, per, capacity).transpose(0, 2, 1, 3)
    chunks = chunks.reshape(peers, 1, PARAMS * capacity)
    moved = lax.all_to_all(chunks, PEERS, split_axis=0, concat_axis=0, tiled=True)
    moved = moved.reshape(rows, per, PARAMS, capacity).transpose(0, 2, 1, 3)
    return moved.reshape(rows, 1, ROW)


VMEM = pl.BlockSpec(memory_space=pltpu.VMEM)
SMEM = pl.BlockSpec(memory_space=pltpu.SMEM)
HBM = pl.BlockSpec(memory_space=pltpu.HBM)
LIMIT = pltpu.CompilerParams(vmem_limit_bytes=40 * 1024 * 1024)


def shards(
    centres,
    log_scales,
    rotations,
    opacity_logits,
    colours,
    view_shift,
    tile_ids,
    tile_counts,
    tile_lists,
    send_index,
    image_cot,
):
    owned = centres.shape[1]
    rows = owned // 128
    peers, capacity = send_index.shape[1:]
    tiles, length = tile_lists.shape
    views = view_shift.shape[0]
    tiles_view = tiles * peers // views
    half_height = 8.0 * (tiles_view // TILES_X)
    assert peers * capacity == owned
    logits = opacity_logits.reshape(rows, 128)
    targets = send_index[0] if capacity % 128 == 0 else send_index.reshape(rows, 128)
    table_shape = jax.ShapeDtypeStruct((rows, 1, ROW), F32)
    whole = jax.ShapeDtypeStruct((rows, 128), jnp.int32)
    outgoing, inverse, view, raw, slots, cot = pl.pallas_call(
        lambda *refs: pre_kernel(half_height, *refs),
        out_shape=(
            table_shape,
            whole,
            whole,
            jax.ShapeDtypeStruct((14 * rows, 128), F32),
            jax.ShapeDtypeStruct((tiles * length // 128, 128), jnp.int32),
            jax.ShapeDtypeStruct(image_cot.shape, F32),
        ),
        in_specs=[SMEM] + [HBM] * 8,
        out_specs=(VMEM,) * 6,
        scratch_shapes=[pltpu.VMEM((n, owned), F32) for n in (3, 3, 4, 3)]
        + [
            pltpu.VMEM(targets.shape, jnp.int32),
            pltpu.VMEM(tile_lists.shape, jnp.int32),
            pltpu.VMEM((rows, 128), jnp.int32),
            pltpu.VMEM((PARAMS * rows, 128), F32),
            pltpu.SemaphoreType.DMA((8,)),
        ],
        compiler_params=LIMIT,
        name="project_and_pack",
    )(
        view_shift,
        centres,
        log_scales,
        rotations,
        logits,
        colours,
        targets,
        tile_lists,
        image_cot,
    )
    received = exchange(outgoing, peers, capacity)
    rendered, slot_grads = pl.pallas_call(
        lambda *refs: render_kernel(tiles_view, length, *refs),
        out_shape=(jax.ShapeDtypeStruct((3, tiles * 256), F32), table_shape),
        in_specs=[SMEM] * 2 + [VMEM] * 3,
        out_specs=(VMEM,) * 2,
        scratch_shapes=[pltpu.VMEM((PARAMS, tiles * length // 1024, 8, 128), F32)]
        + [pltpu.VMEM((tiles * length // 8, 128), F32)] * 3
        + [pltpu.VMEM((PARAMS * rows, 128), F32)]
        + [
            pltpu.VMEM((length, 256), F32),
            pltpu.VMEM((length, 256), F32),
            pltpu.VMEM((length, 512), BF16),
            pltpu.VMEM((length, 512), BF16),
        ]
        * 2,
        compiler_params=LIMIT,
        name="render",
    )(tile_counts, tile_ids, received, slots, cot)
    returned = exchange(slot_grads, peers, capacity)
    shapes = [jax.ShapeDtypeStruct((n, owned), F32) for n in (3, 3, 4, 3)]
    shapes.insert(3, jax.ShapeDtypeStruct((rows, 128), F32))
    grads = pl.pallas_call(
        lambda *refs: post_kernel(half_height, *refs),
        out_shape=tuple(shapes),
        in_specs=[SMEM] + [VMEM] * 4,
        out_specs=(VMEM,) * 5,
        scratch_shapes=[
            pltpu.VMEM((PARAMS, rows, 128), F32),
            pltpu.VMEM((13 * rows, 128), F32),
        ],
        compiler_params=LIMIT,
        name="unpack_and_project_back",
    )(view_shift, raw, inverse, view, returned)
    return (rendered, grads[0], grads[1], grads[2], grads[3].reshape(owned), grads[4])


def solution(mesh):
    wide = P(None, AXES)
    flat = P(AXES)
    return jax.shard_map(
        shards,
        mesh=mesh,
        in_specs=(
            wide,
            wide,
            wide,
            flat,
            wide,
            P("groups", None),
            flat,
            flat,
            P(AXES, None),
            P(AXES, None, None),
            wide,
        ),
        out_specs=(wide, wide, wide, wide, flat, wide),
        check_vma=False,
    )
```

time: 88 us -> 65.1 us (0.74)
  Pallas kernels: 54.7 us -> 29.9 us
  local copies, waits for them, and re-layouts: 5.51 us -> 7.73 us
    pallas_call x2, Pallas kernels: 49.3 us -> 26.4 us  [the longest x1 22.3 us: shards(): pl.pallas_call(lambda *refs: render_kernel(tiles_view, length, *refs), ou...]
    unnamed x32 -> x22, local copies, waits for them, and re-layouts: 5.51 us -> 7.73 us
    pallas_call x1, Pallas kernels: 5.49 us -> 3.52 us  [shards(): pl.pallas_call(lambda *refs: post_kernel(half_height, *refs), out_shape=t...]
where the time goes in v2:
time: 65.1 us; the launch traced here: 64.5 us
  Pallas kernels  29.9 us (46%)
  blocking collectives  26.2 us (40%)
  local copies, waits for them, and re-layouts  7.73 us (12%)
  between operations  0.66 us (1%)
    all_to_all x2, blocking collectives, exchange(): return lax.all_to_all(table, PEERS, split_axis=0, concat_axis=0, tiled=True)  26.2 us
    pallas_call x1, Pallas kernels, shards(): pl.pallas_call(lambda *refs: render_kernel(tiles_view, length, *refs), ou...  22.3 us
    unnamed x22, local copies, waits for them, and re-layouts  7.73 us
    pallas_call x1, Pallas kernels, shards(): pl.pallas_call(lambda *refs: pre_kernel(half_height, *refs), out_shape=(t...  4.12 us
    pallas_call x1, Pallas kernels, shards(): pl.pallas_call(lambda *refs: post_kernel(half_height, *refs), out_shape=t...  3.52 us

profile of v2, /device:TPU:0, one launch (start us, length us, event | category | flops | bytes accessed | tf_op | source)
XLA Modules:
  0.0 64.5 jit_solution(18441125478329252510)
XLA Ops:
  0.6 0.0 copy-start.8
  0.6 0.7 %copy-done.8 = f32[4,3]{1,0:T(4,128)S(1)} copy-done((f32[4,3]{1,0:T(4,128)S(1)}, f32[4,3]{1,0:T(4,128)}, u32[]{:S(2)}) %copy-start.8) | copy-done | bytes 72
  1.3 0.0 copy-start
  1.3 0.8 %copy-done = f32[3,4096]{1,0:T(4,128)S(1)} copy-done((f32[3,4096]{1,0:T(4,128)S(1)}, f32[3,4096]{1,0:T(4,128)}, u32[]{:S(2)}) %copy-start) | copy-done | bytes 49176
  2.2 0.0 copy-start.1
  2.2 0.8 %copy-done.1 = f32[3,4096]{1,0:T(4,128)S(1)} copy-done((f32[3,4096]{1,0:T(4,128)S(1)}, f32[3,4096]{1,0:T(4,128)}, u32[]{:S(2)}) %copy-start.1) | copy-done | bytes 49176
  3.0 0.0 copy-start.2
  3.0 0.8 %copy-done.2 = f32[4,4096]{1,0:T(4,128)S(1)} copy-done((f32[4,4096]{1,0:T(4,128)S(1)}, f32[4,4096]{1,0:T(4,128)}, u32[]{:S(2)}) %copy-start.2) | copy-done | bytes 65560
  3.8 0.0 copy-start.3
  3.8 0.8 %copy-done.3 = f32[3,4096]{1,0:T(4,128)S(1)} copy-done((f32[3,4096]{1,0:T(4,128)S(1)}, f32[3,4096]{1,0:T(4,128)}, u32[]{:S(2)}) %copy-start.3) | copy-done | bytes 49176
  4.7 0.0 copy-start.4
  4.7 0.8 %copy-done.4 = f32[3,4096]{1,0:T(4,128)S(1)} copy-done((f32[3,4096]{1,0:T(4,128)S(1)}, f32[3,4096]{1,0:T(4,128)}, u32[]{:S(2)}) %copy-start.4) | copy-done | bytes 49176
  5.5 0.0 copy-start.5
  5.5 0.8 %copy-done.5 = s32[16,512]{1,0:T(8,128)S(1)} copy-done((s32[16,512]{1,0:T(8,128)S(1)}, s32[16,512]{1,0:T(8,128)}, u32[]{:S(2)}) %copy-start.5) | copy-done | bytes 32792
  6.3 0.7 %copy-done.6 = f32[4096]{0:T(1024)S(1)} copy-done((f32[4096]{0:T(1024)S(1)}, f32[4096]{0:T(1024)}, u32[]{:S(2)}) %copy-start.6) | copy-done | bytes 16408
  7.0 0.0 copy-start.7
  7.0 0.7 %copy-done.7 = s32[1,16,256]{2,1,0:T(8,128)S(1)} copy-done((s32[1,16,256]{2,1,0:T(8,128)S(1)}, s32[1,16,256]{2,1,0:T(8,128)}, u32[]{:S(2)}) %copy-start.7) | copy-done | bytes 16408
  7.7 4.1 %project_and_pack.1 = (f32[32,1,1152]{2,1,0:T(1,128)S(1)}, s32[32,128]{1,0:T(8,128)S(1)}, s32[32,128]{1,0:T(8,128)S(1)}, f32[448,128]{1,0:T(8,128)S(1)}, s32[64,128]{1,0:T(8,128)S(1)}, /*index=5*/f32[3,4096]{1,0:T(4,128)S(1)}) custom-call(f32[4,3]{1,0:T(4,128)S(1)} %copy-done.8, f32[3,4096]{1,0:T(4,128)S(1)} %copy-done, f32[3,4096]{1,0:T(4,128)S(1)} %copy-done.1, ...), custom_call_target="tpu_custom_call" | custom-call | tf_op jit(solution)/shard_map/project_and_pack/pallas_call | solution.py:584
  11.8 15.4 %all_to_all.10.refs_2_ = f32[32,1,1152]{2,1,0:T(1,128)S(1)} all-to-all(f32[32,1,1152]{2,1,0:T(1,128)S(1)} %get-tuple-element.19), channel_id=1, replica_groups=mesh['groups'=2,'gs'=8,'sub'=2] {'gs','sub'}, dimensions={0} | all-to-all | bytes 294912 | tf_op jit(solution)/shard_map/all_to_all | solution.py:543
  27.2 0.7 %copy-done.9 = s32[16]{0:T(128)S(1)} copy-done((s32[16]{0:T(128)S(1)}, s32[16]{0:T(128)}, u32[]{:S(2)}) %copy-start.9) | copy-done | bytes 88
  27.9 0.0 copy-done.10
  27.9 22.3 %render.1 = (f32[3,4096]{1,0:T(4,128)}, f32[32,1,1152]{2,1,0:T(1,128)S(1)}) custom-call(s32[16]{0:T(128)S(1)} %copy-done.9, s32[16]{0:T(128)S(1)} %copy-done.10, f32[32,1,1152]{2,1,0:T(1,128)S(1)} %all_to_all.10.refs_2_, s32[64,128]{1,0:T(8,128)S(1)} %get-tuple-element.20.refs_3_, f32[3,4096]{1,0:T(4,128)S(1)} %get-tuple-element.21.refs_4_), custom_call_target="tpu_custom_call" | custom-call | tf_op jit(solution)/shard_map/render/pallas_call | solution.py:618
  50.2 10.8 %all_to_all.11.refs_4_ = f32[32,1,1152]{2,1,0:T(1,128)S(1)} all-to-all(f32[32,1,1152]{2,1,0:T(1,128)S(1)} %get-tuple-element.26), channel_id=1, replica_groups=mesh['groups'=2,'gs'=8,'sub'=2] {'gs','sub'}, dimensions={0} | all-to-all | bytes 294912 | tf_op jit(solution)/shard_map/all_to_all | solution.py:543
  60.9 3.5 %unpack_and_project_back.1 = (f32[3,4096]{1,0:T(4,128)}, f32[3,4096]{1,0:T(4,128)}, f32[4,4096]{1,0:T(4,128)}, f32[32,128]{1,0:T(8,128)}, f32[3,4096]{1,0:T(4,128)}) custom-call(f32[4,3]{1,0:T(4,128)S(1)} %copy-done.8, f32[448,128]{1,0:T(8,128)S(1)} %get-tuple-element.23.refs_1_, s32[32,128]{1,0:T(8,128)S(1)} %get-tuple-element.24.refs_2_, ...), custom_call_target="tpu_custom_call" | custom-call | tf_op jit(solution)/shard_map/unpack_and_project_back/pallas_call | solution.py:639
  (3 shorter events, 0.0 us)
Async XLA Ops:
  0.6 0.7 %copy-start.8 = (f32[4,3]{1,0:T(4,128)S(1)}, f32[4,3]{1,0:T(4,128)}, u32[]{:S(2)}) copy-start(f32[4,3]{1,0:T(4,128)} %refs_0_.5) | copy-start | bytes 148
  1.3 0.8 %copy-start = (f32[3,4096]{1,0:T(4,128)S(1)}, f32[3,4096]{1,0:T(4,128)}, u32[]{:S(2)}) copy-start(f32[3,4096]{1,0:T(4,128)} %refs_1_.2) | copy-start | bytes 147460
  2.2 0.8 %copy-start.1 = (f32[3,4096]{1,0:T(4,128)S(1)}, f32[3,4096]{1,0:T(4,128)}, u32[]{:S(2)}) copy-start(f32[3,4096]{1,0:T(4,128)} %refs_2_.1) | copy-start | bytes 147460
  3.0 0.8 %copy-start.2 = (f32[4,4096]{1,0:T(4,128)S(1)}, f32[4,4096]{1,0:T(4,128)}, u32[]{:S(2)}) copy-start(f32[4,4096]{1,0:T(4,128)} %refs_3_.1) | copy-start | bytes 196612
  3.8 0.8 %copy-start.3 = (f32[3,4096]{1,0:T(4,128)S(1)}, f32[3,4096]{1,0:T(4,128)}, u32[]{:S(2)}) copy-start(f32[3,4096]{1,0:T(4,128)} %refs_5_.1) | copy-start | bytes 147460
  4.7 0.8 %copy-start.4 = (f32[3,4096]{1,0:T(4,128)S(1)}, f32[3,4096]{1,0:T(4,128)}, u32[]{:S(2)}) copy-start(f32[3,4096]{1,0:T(4,128)} %refs_8_.1) | copy-start | bytes 147460
  5.5 0.8 %copy-start.5 = (s32[16,512]{1,0:T(8,128)S(1)}, s32[16,512]{1,0:T(8,128)}, u32[]{:S(2)}) copy-start(s32[16,512]{1,0:T(8,128)} %refs_7_.1) | copy-start | bytes 98308
  6.3 0.7 %copy-start.6 = (f32[4096]{0:T(1024)S(1)}, f32[4096]{0:T(1024)}, u32[]{:S(2)}) copy-start(f32[4096]{0:T(1024)} %param.14) | copy-start | bytes 49156
  7.0 0.7 %copy-start.7 = (s32[1,16,256]{2,1,0:T(8,128)S(1)}, s32[1,16,256]{2,1,0:T(8,128)}, u32[]{:S(2)}) copy-start(s32[1,16,256]{2,1,0:T(8,128)} %param.20) | copy-start | bytes 49156
  27.2 0.7 %copy-start.9 = (s32[16]{0:T(128)S(1)}, s32[16]{0:T(128)}, u32[]{:S(2)}) copy-start(s32[16]{0:T(128)} %refs_0_.4) | copy-start | bytes 196
  27.2 0.7 %copy-start.10 = (s32[16]{0:T(128)S(1)}, s32[16]{0:T(128)}, u32[]{:S(2)}) copy-start(s32[16]{0:T(128)} %refs_1_.3) | copy-start | bytes 196

commit v3 on v2

--- a/solution.py
+++ b/solution.py
@@ -141,7 +141,10 @@
 
 def pre_kernel(
     half_height,
+    tiles_view,
     shift_ref,
+    count_ref,
+    id_ref,
     centre_hbm,
     scale_hbm,
     rotation_hbm,
@@ -149,13 +152,12 @@
     colour_hbm,
     send_hbm,
     list_hbm,
-    cot_hbm,
     out_ref,
     inverse_ref,
     view_ref,
     raw,
     slots,
-    cot_ref,
+    marks,
     centre_ref,
     scale_ref,
     rotation_ref,
@@ -177,7 +179,6 @@
         (colour_hbm, colour_ref),
         (logit_hbm, logit_ref),
         (list_hbm, list_ref),
-        (cot_hbm, cot_ref),
     ]
     copies = [
         pltpu.make_async_copy(source, target, arrived.at[i])
@@ -253,7 +254,10 @@
                 )
                 moved = jnp.where(entry >> 7 == source, taken, moved)
             slots[pl.ds(i * 8 * blocks + b, 8, stride=blocks), :] = moved
-    copies[7].wait()
+    for t in range(tiles):
+        local = lax.rem(id_ref[t], tiles_view)
+        mark = count_ref[t] + 1024 * local
+        marks[t * blocks : t * blocks + blocks, :] = jnp.full((blocks, 128), mark, jnp.int32)
 
 
 def run_entry(lane, block, length):
@@ -261,12 +265,10 @@
 
 
 def render_kernel(
-    tiles_view,
     length,
-    count_ref,
-    id_ref,
     table_ref,
     slots,
+    marks,
     cot_ref,
     image_ref,
     grad_ref,
@@ -280,58 +282,11 @@
     blocks = length // 128
     tiles = slots.shape[0] // blocks
     rows = table_ref.shape[0]
-    places = [(8 * i, b) for i in range(tiles // 8) for b in range(blocks)]
-    stride = 16 * blocks
-
-    def spot(first, b, k):
-        return pl.ds((first * blocks + b) * 16 + k, 8, stride=stride)
-
-    index = [slots[pl.ds(first * blocks + b, 8, stride=blocks), :] for first, b in places]
-
-    def gather(c, carry):
-        offset = pl.multiple_of(c * 128, 128)
-        for pos, value in enumerate(index):
-            gathered[c, pos] = lookup(
-                lambda row: table_ref[row, :, pl.ds(offset, 128)], value, rows
-            )
-        return carry
-
-    lax.fori_loop(0, PARAMS, gather, 0)
-
-    sublane = iota((8, 128), 0)
+    group = 8 // blocks
+    steps = length // 16
+    groups = tiles // group
     lane = iota((8, 128), 1)
-    mid_x, mid_y, live = [], [], []
-    for i in range(tiles // 8):
-        x = jnp.zeros((8, 128), jnp.int32)
-        y = x
-        n = x
-        for s in range(8):
-            local = lax.rem(id_ref[i * 8 + s], tiles_view)
-            x = jnp.where(sublane == s, 16 * lax.rem(local, TILES_X) + 8, x)
-            y = jnp.where(sublane == s, 16 * lax.div(local, TILES_X) + 8, y)
-            n = jnp.where(sublane == s, count_ref[i * 8 + s], n)
-        mid_x.append(x.astype(F32))
-        mid_y.append(y.astype(F32))
-        live.append(n)
-
-    def entry(pos):
-        u, w, a, b, e, o = [gathered[c, pos] for c in range(6)]
-        first = places[pos][0]
-        return u - mid_x[first // 8], w - mid_y[first // 8], a, b, e, o
-
-    coefs[...] = jnp.zeros(coefs.shape, F32)
-    for pos, (first, block) in enumerate(places):
-        du, dw, a, b, e, o = entry(pos)
-        is_live = run_entry(lane, block, length) < live[first // 8]
-        slope_x = a * du + b * dw
-        slope_y = e * dw + b * du
-        level = -0.5 * (du * slope_x + dw * slope_y) + jnp.log(o)
-        values = [-0.5 * a, -0.5 * e, -b, slope_x, slope_y, level]
-        for k, value in enumerate(values):
-            dead = -1000.0 if k == 5 else 0.0
-            coefs[spot(first, block, k), :] = jnp.where(is_live, value * LOG2E, dead)
-        for k in range(3):
-            coefs[spot(first, block, 8 + k), :] = gathered[6 + k, pos] - BACKGROUND
+    block_of = iota((8, 128), 0) % blocks
 
     feature = iota((8, 256), 0)
     pixel = iota((8, 256), 1)
@@ -357,7 +312,77 @@
             value = value + jnp.where(run_row < 8 - step, moved, 0.0)
         return jnp.where(run_row < 7, pltpu.roll(value, 7, 0), 0.0)
 
-    def render(t, alpha_ref, share_ref, weights, slopes):
+    def spread(k):
+        return pl.ds(k, 8, stride=16)
+
+    def placed(g, params):
+        u, w, a, b, e, o = params
+        mark = marks[pl.ds(pl.multiple_of(g * 8, 8), 8), :]
+        local = mark >> 10
+        mid_x = (16 * lax.rem(local, TILES_X) + 8).astype(F32)
+        mid_y = (16 * lax.div(local, TILES_X) + 8).astype(F32)
+        return u - mid_x, w - mid_y, a, b, e, o, mark & 1023
+
+    def gather(g):
+        index = slots[pl.ds(pl.multiple_of(g * 8, 8), 8), :]
+        low = index & 127
+        high = index >> 7
+        found = [jnp.zeros((8, 128), F32)] * PARAMS
+        for row in range(rows):
+            is_row = high == row
+            for c in range(PARAMS):
+                value = jnp.broadcast_to(table_ref[row, :, c * 128 : c * 128 + 128], (8, 128))
+                value = jnp.take_along_axis(value, low, axis=1, mode="promise_in_bounds")
+                found[c] = jnp.where(is_row, value, found[c])
+        for c in range(6):
+            gathered[g, c] = found[c]
+        du, dw, a, b, e, o, live = placed(g, found[:6])
+        entry = (lane & 7) * (length // 8) + block_of * 16 + (lane >> 3)
+        is_live = entry < live
+        slope_x = a * du + b * dw
+        slope_y = e * dw + b * du
+        level = -0.5 * (du * slope_x + dw * slope_y) + jnp.log(o)
+        values = [-0.5 * a, -0.5 * e, -b, slope_x, slope_y, level]
+        for k, value in enumerate(values):
+            dead = -1000.0 if k == 5 else 0.0
+            coefs[spread(k), :] = jnp.where(is_live, value * LOG2E, dead)
+        for k in range(3):
+            coefs[spread(8 + k), :] = found[6 + k] - BACKGROUND
+
+    def chain(g):
+        du, dw, a, b, e, o, _ = placed(g, [gathered[g, c] for c in range(6)])
+        m_xx, m_yy, m_xy, m_x, m_y, m_one = [moments[spread(k), :] for k in range(6)]
+        d_x = m_x - du * m_one
+        d_y = m_y - dw * m_one
+        values = [
+            a * d_x + b * d_y,
+            e * d_y + b * d_x,
+            -0.5 * (m_xx - du * (m_x + d_x)),
+            -(m_xy - dw * m_x - du * d_y),
+            -0.5 * (m_yy - dw * (m_y + d_y)),
+            m_one / o,
+        ] + [moments[spread(8 + k), :] for k in range(3)]
+        for c, value in enumerate(values):
+            high = value.astype(BF16).astype(F32)
+            grads[2 * c] = high
+            grads[2 * c + 1] = value - high
+
+    def scatter(g):
+        index = slots[pl.ds(pl.multiple_of(g * 8, 8), 8), :]
+        lefts, rights = [], []
+        for r in range(8):
+            slot = index[r : r + 1, :]
+            match = jnp.broadcast_to(slot >> 8, (rows // 2, 128)) == iota((rows // 2, 128), 0)
+            where = jnp.broadcast_to(slot & 255, (256, 128)) == iota((256, 128), 0)
+            rights.append(jnp.where(where, 1.0, 0.0).astype(BF16))
+            parts = [
+                jnp.where(match, jnp.broadcast_to(grads[c, r : r + 1, :], match.shape), 0.0)
+                for c in range(2 * PARAMS)
+            ]
+            lefts.append(jnp.concatenate(parts, 0).astype(BF16))
+        slot_ref[...] += dot(jnp.concatenate(lefts, 1), jnp.concatenate(rights, 1), NT)
+
+    def operands(t, i):
         lanes = pl.ds(pl.multiple_of(t * 256, 256), 256)
         cot = jnp.concatenate([cot_ref[:, lanes], jnp.zeros((5, 256), F32)], 0)
         cot_high = cot.astype(BF16).astype(F32)
@@ -373,9 +398,9 @@
         cot_rows = jnp.concatenate([cot_rows, cot_rows], 1).astype(BF16)
         lefts, tints = [], []
         for b in range(blocks):
-            base = pl.multiple_of((t * blocks + b) * 16, 16)
-            coef = coefs[pl.ds(base, 8), :]
-            tint = coefs[pl.ds(base + 8, 8), :]
+            base = (i * blocks + b) * 16
+            coef = coefs[base : base + 8, :]
+            tint = coefs[base + 8 : base + 16, :]
             coef_high = coef.astype(BF16).astype(F32)
             rest = coef - coef_high
             coef_mid = rest.astype(BF16).astype(F32)
@@ -389,8 +414,9 @@
             tints.append(jnp.concatenate([tint_high, tint_low], 0))
         left = jnp.concatenate(lefts, 1).astype(BF16)
         tint_rows = jnp.concatenate(tints, 1).astype(BF16)
-        both = dot(left, right, TN)
-        steps = length // 16
+        return lanes, cot_rows, tint_rows, dot(left, right, TN)
+
+    def render(i, lanes, cot_rows, tint_rows, both, alpha_ref, share_ref, weights, slopes):
         left_over = jnp.ones((8, 256), F32)
         for step in range(steps):
             here = slice(step * 16, step * 16 + 16)
@@ -433,63 +459,37 @@
             slopes[here, 256:] = low
         summed = dot(moment_rows, slopes[...], NT)
         for b in range(blocks):
-            base = pl.multiple_of((t * blocks + b) * 16, 16)
+            base = (i * blocks + b) * 16
             here = slice(b * 128, b * 128 + 128)
-            moments[pl.ds(base, 8), :] = summed[:8, here]
-            moments[pl.ds(base + 8, 8), :] = tint_grad[:, here]
-
-    def pair(t, carry):
-        render(2 * t, *buffers[:4])
-        render(2 * t + 1, *buffers[4:])
+            moments[base : base + 8, :] = summed[:8, here]
+            moments[base + 8 : base + 16, :] = tint_grad[:, here]
+
+    slot_ref[...] = jnp.zeros(slot_ref.shape, F32)
+    moments[...] = jnp.zeros(moments.shape, F32)
+    coefs[...] = jnp.zeros(coefs.shape, F32)
+    gather(0)
+
+    def step(g, carry):
+        before = jnp.maximum(g - 1, 0)
+        chain(before)
+        ready = [operands(g * group + i, i) for i in range(group)]
+        gather(jnp.minimum(g + 1, groups - 1))
+        scatter(before)
+        for i in range(group):
+            render(i, *ready[i], *buffers[4 * i : 4 * i + 4])
         return carry
 
-    lax.fori_loop(0, tiles // 2, pair, 0)
-
-    for pos, (first, block) in enumerate(places):
-        du, dw, a, b, e, o = entry(pos)
-        m_xx, m_yy, m_xy, m_x, m_y, m_one = [moments[spot(first, block, k), :] for k in range(6)]
-        d_x = m_x - du * m_one
-        d_y = m_y - dw * m_one
-        values = [
-            a * d_x + b * d_y,
-            e * d_y + b * d_x,
-            -0.5 * (m_xx - du * (m_x + d_x)),
-            -(m_xy - dw * m_x - du * d_y),
-            -0.5 * (m_yy - dw * (m_y + d_y)),
-            m_one / o,
-        ] + [moments[spot(first, block, 8 + k), :] for k in range(3)]
-        for k, value in enumerate(values):
-            grads[spot(first, block, k), :] = value
-
-    slot_ref[...] = jnp.zeros(slot_ref.shape, F32)
-
-    def scatter(t, carry):
-        lefts, rights = [], []
-        for b in range(blocks):
-            base = pl.multiple_of((t * blocks + b) * 16, 16)
-            entry_slot = slots[pl.ds(t * blocks + b, 1), :]
-            match = jnp.broadcast_to(entry_slot >> 7, (rows, 128)) == iota((rows, 128), 0)
-            where = jnp.broadcast_to(entry_slot & 127, (128, 128)) == iota((128, 128), 0)
-            right = jnp.where(where, 1.0, 0.0).astype(BF16)
-            high_rows, low_rows = [], []
-            for c in range(PARAMS):
-                value = grads[pl.ds(base + c, 1), :]
-                value_high = value.astype(BF16).astype(F32)
-                high_rows.append(jnp.where(match, value_high, 0.0))
-                low_rows.append(jnp.where(match, value - value_high, 0.0))
-            lefts.append(jnp.concatenate(high_rows, 0).astype(BF16))
-            lefts.append(jnp.concatenate(low_rows, 0).astype(BF16))
-            rights += [right, right]
-        slot_ref[...] += dot(jnp.concatenate(lefts, 1), jnp.concatenate(rights, 1), NT)
-        return carry
-
-    lax.fori_loop(0, tiles, scatter, 0)
-
+    lax.fori_loop(0, groups, step, 0)
+    chain(groups - 1)
+    scatter(groups - 1)
+
+    half = rows // 2
     for c in range(PARAMS):
+        high = slot_ref[2 * c * half : (2 * c + 1) * half, :]
+        value = high + slot_ref[(2 * c + 1) * half : (2 * c + 2) * half, :]
         for row in range(rows):
-            grad_ref[row, :, c * 128 : c * 128 + 128] = slot_ref[
-                c * rows + row : c * rows + row + 1, :
-            ]
+            part = value[row // 2 : row // 2 + 1, row % 2 * 128 : row % 2 * 128 + 128]
+            grad_ref[row, :, c * 128 : c * 128 + 128] = part
 
 
 def post_kernel(
@@ -554,6 +554,7 @@
 SMEM = pl.BlockSpec(memory_space=pltpu.SMEM)
 HBM = pl.BlockSpec(memory_space=pltpu.HBM)
 LIMIT = pltpu.CompilerParams(vmem_limit_bytes=40 * 1024 * 1024)
+FULL = pltpu.CompilerParams(vmem_limit_bytes=60 * 1024 * 1024)
 
 
 def shards(
@@ -581,17 +582,18 @@
     targets = send_index[0] if capacity % 128 == 0 else send_index.reshape(rows, 128)
     table_shape = jax.ShapeDtypeStruct((rows, 1, ROW), F32)
     whole = jax.ShapeDtypeStruct((rows, 128), jnp.int32)
-    outgoing, inverse, view, raw, slots, cot = pl.pallas_call(
-        lambda *refs: pre_kernel(half_height, *refs),
+    entry_shape = jax.ShapeDtypeStruct((tiles * length // 128, 128), jnp.int32)
+    outgoing, inverse, view, raw, slots, marks = pl.pallas_call(
+        lambda *refs: pre_kernel(half_height, tiles_view, *refs),
         out_shape=(
             table_shape,
             whole,
             whole,
             jax.ShapeDtypeStruct((14 * rows, 128), F32),
-            jax.ShapeDtypeStruct((tiles * length // 128, 128), jnp.int32),
-            jax.ShapeDtypeStruct(image_cot.shape, F32),
+            entry_shape,
+            entry_shape,
         ),
-        in_specs=[SMEM] + [HBM] * 8,
+        in_specs=[SMEM] * 3 + [HBM] * 7,
         out_specs=(VMEM,) * 6,
         scratch_shapes=[pltpu.VMEM((n, owned), F32) for n in (3, 3, 4, 3)]
         + [
@@ -599,12 +601,14 @@
             pltpu.VMEM(tile_lists.shape, jnp.int32),
             pltpu.VMEM((rows, 128), jnp.int32),
             pltpu.VMEM((PARAMS * rows, 128), F32),
-            pltpu.SemaphoreType.DMA((8,)),
+            pltpu.SemaphoreType.DMA((7,)),
         ],
-        compiler_params=LIMIT,
+        compiler_params=FULL,
         name="project_and_pack",
     )(
         view_shift,
+        tile_counts,
+        tile_ids,
         centres,
         log_scales,
         rotations,
@@ -612,27 +616,30 @@
         colours,
         targets,
         tile_lists,
-        image_cot,
     )
     received = exchange(outgoing, peers, capacity)
     rendered, slot_grads = pl.pallas_call(
-        lambda *refs: render_kernel(tiles_view, length, *refs),
+        lambda *refs: render_kernel(length, *refs),
         out_shape=(jax.ShapeDtypeStruct((3, tiles * 256), F32), table_shape),
-        in_specs=[SMEM] * 2 + [VMEM] * 3,
+        in_specs=[VMEM] * 4,
         out_specs=(VMEM,) * 2,
-        scratch_shapes=[pltpu.VMEM((PARAMS, tiles * length // 1024, 8, 128), F32)]
-        + [pltpu.VMEM((tiles * length // 8, 128), F32)] * 3
-        + [pltpu.VMEM((PARAMS * rows, 128), F32)]
+        scratch_shapes=[
+            pltpu.VMEM((tiles * length // 1024, 6, 8, 128), F32),
+            pltpu.VMEM((128, 128), F32),
+            pltpu.VMEM((128, 128), F32),
+            pltpu.VMEM((2 * PARAMS, 8, 128), F32),
+            pltpu.VMEM((PARAMS * rows, 256), F32),
+        ]
         + [
             pltpu.VMEM((length, 256), F32),
             pltpu.VMEM((length, 256), F32),
             pltpu.VMEM((length, 512), BF16),
             pltpu.VMEM((length, 512), BF16),
         ]
-        * 2,
+        * (1024 // length),
         compiler_params=LIMIT,
         name="render",
-    )(tile_counts, tile_ids, received, slots, cot)
+    )(received, slots, marks, image_cot)
     returned = exchange(slot_grads, peers, capacity)
     shapes = [jax.ShapeDtypeStruct((n, owned), F32) for n in (3, 3, 4, 3)]
     shapes.insert(3, jax.ShapeDtypeStruct((rows, 128), F32))

time: 65.1 us -> 49.8 us (0.76)
  Pallas kernels: 29.9 us -> 21.4 us
  local copies, waits for them, and re-layouts: 7.73 us -> 0.71 us
    pallas_call x2, Pallas kernels: 26.4 us -> 17.9 us  [the longest x1 12.8 us: shards(): pl.pallas_call(lambda *refs: render_kernel(length, *refs), out_shape=(jax...]
    unnamed x22 -> x14, local copies, waits for them, and re-layouts: 7.73 us -> 0.71 us
where the time goes in v3:
time: 49.8 us; the launch traced here: 49.4 us
  blocking collectives  26.5 us (53%)
  Pallas kernels  21.4 us (43%)
  local copies, waits for them, and re-layouts  0.71 us (1%)
  between operations  0.71 us (1%)
    all_to_all x2, blocking collectives, exchange(): return lax.all_to_all(table, PEERS, split_axis=0, concat_axis=0, tiled=True)  26.5 us
    pallas_call x1, Pallas kernels, shards(): pl.pallas_call(lambda *refs: render_kernel(length, *refs), out_shape=(jax...  12.8 us
    pallas_call x1, Pallas kernels, shards(): pl.pallas_call(lambda *refs: pre_kernel(half_height, tiles_view, *refs),...  5.1 us
    pallas_call x1, Pallas kernels, shards(): pl.pallas_call(lambda *refs: post_kernel(half_height, *refs), out_shape=t...  3.52 us

profile of v3, /device:TPU:0, one launch (start us, length us, event | category | flops | bytes accessed | tf_op | source)
XLA Modules:
  0.0 49.4 jit_solution(8022104390975402551)
XLA Ops:
  0.6 5.1 %project_and_pack.1 = (f32[32,1,1152]{2,1,0:T(1,128)}, s32[32,128]{1,0:T(8,128)}, s32[32,128]{1,0:T(8,128)}, f32[448,128]{1,0:T(8,128)}, s32[64,128]{1,0:T(8,128)}, /*index=5*/s32[64,128]{1,0:T(8,128)}) custom-call(f32[4,3]{1,0:T(4,128)} %refs_0_.3, s32[16]{0:T(128)} %refs_1_.1, s32[16]{0:T(128)} %refs_2_.1, f32[3,4096]{1,0:T(4,128)} %refs_3_.2, ...), custom_call_target="tpu_custom_call" | custom-call | tf_op jit(solution)/shard_map/project_and_pack/pallas_call | solution.py:586
  5.7 0.0 copy-start.1
  5.8 0.0 copy-start.2
  5.8 0.0 copy-start.3
  5.8 15.7 %all_to_all.10.refs_0_ = f32[32,1,1152]{2,1,0:T(1,128)S(1)} all-to-all(f32[32,1,1152]{2,1,0:T(1,128)} %get-tuple-element.19), channel_id=1, replica_groups=mesh['groups'=2,'gs'=8,'sub'=2] {'gs','sub'}, dimensions={0} | all-to-all | bytes 294912 | tf_op jit(solution)/shard_map/all_to_all | solution.py:543
  21.5 0.0 copy-done.1
  21.5 0.0 copy-done.2
  21.5 0.0 copy-done.3
  21.5 0.0 copy-start
  21.5 12.8 %render.1 = (f32[3,4096]{1,0:T(4,128)}, f32[32,1,1152]{2,1,0:T(1,128)S(1)}) custom-call(f32[32,1,1152]{2,1,0:T(1,128)S(1)} %all_to_all.10.refs_0_, s32[64,128]{1,0:T(8,128)S(1)} %copy-done.2, s32[64,128]{1,0:T(8,128)S(1)} %copy-done.3, f32[3,4096]{1,0:T(4,128)S(1)} %copy-done.1), custom_call_target="tpu_custom_call" | custom-call | tf_op jit(solution)/shard_map/render/pallas_call | solution.py:621
  34.3 0.0 copy-start.4
  34.4 0.0 copy-start.5
  34.4 10.8 %all_to_all.11.refs_4_ = f32[32,1,1152]{2,1,0:T(1,128)S(1)} all-to-all(f32[32,1,1152]{2,1,0:T(1,128)S(1)} %get-tuple-element.26), channel_id=1, replica_groups=mesh['groups'=2,'gs'=8,'sub'=2] {'gs','sub'}, dimensions={0} | all-to-all | bytes 294912 | tf_op jit(solution)/shard_map/all_to_all | solution.py:543
  45.2 0.0 copy-start.6
  45.2 0.0 copy-done
  45.2 0.0 copy-done.4
  45.2 0.0 copy-done.5
  45.2 0.7 %copy-done.6 = f32[4,3]{1,0:T(4,128)S(1)} copy-done((f32[4,3]{1,0:T(4,128)S(1)}, f32[4,3]{1,0:T(4,128)}, u32[]{:S(2)}) %copy-start.6) | copy-done | bytes 72
  45.8 3.5 %unpack_and_project_back.1 = (f32[3,4096]{1,0:T(4,128)}, f32[3,4096]{1,0:T(4,128)}, f32[4,4096]{1,0:T(4,128)}, f32[32,128]{1,0:T(8,128)}, f32[3,4096]{1,0:T(4,128)}) custom-call(f32[4,3]{1,0:T(4,128)S(1)} %copy-done.6, f32[448,128]{1,0:T(8,128)S(1)} %copy-done, s32[32,128]{1,0:T(8,128)S(1)} %copy-done.4, s32[32,128]{1,0:T(8,128)S(1)} %copy-done.5, ...), custom_call_target="tpu_custom_call" | custom-call | tf_op jit(solution)/shard_map/unpack_and_project_back/pallas_call | solution.py:646
Async XLA Ops:
  5.7 15.8 %copy-start.1 = (f32[3,4096]{1,0:T(4,128)S(1)}, f32[3,4096]{1,0:T(4,128)}, u32[]{:S(2)}) copy-start(f32[3,4096]{1,0:T(4,128)} %refs_3_.3) | copy-start | bytes 147460
  5.8 15.8 %copy-start.2 = (s32[64,128]{1,0:T(8,128)S(1)}, s32[64,128]{1,0:T(8,128)}, u32[]{:S(2)}) copy-start(s32[64,128]{1,0:T(8,128)} %get-tuple-element.20.refs_1_) | copy-start | bytes 98308
  5.8 15.7 %copy-start.3 = (s32[64,128]{1,0:T(8,128)S(1)}, s32[64,128]{1,0:T(8,128)}, u32[]{:S(2)}) copy-start(s32[64,128]{1,0:T(8,128)} %get-tuple-element.21.refs_2_) | copy-start | bytes 98308
  21.5 23.7 %copy-start = (f32[448,128]{1,0:T(8,128)S(1)}, f32[448,128]{1,0:T(8,128)}, u32[]{:S(2)}) copy-start(f32[448,128]{1,0:T(8,128)} %get-tuple-element.23.refs_1_) | copy-start | bytes 688132
  34.3 10.8 %copy-start.4 = (s32[32,128]{1,0:T(8,128)S(1)}, s32[32,128]{1,0:T(8,128)}, u32[]{:S(2)}) copy-start(s32[32,128]{1,0:T(8,128)} %get-tuple-element.24.refs_2_) | copy-start | bytes 49156
  34.4 10.8 %copy-start.5 = (s32[32,128]{1,0:T(8,128)S(1)}, s32[32,128]{1,0:T(8,128)}, u32[]{:S(2)}) copy-start(s32[32,128]{1,0:T(8,128)} %get-tuple-element.25.refs_3_) | copy-start | bytes 49156
  45.2 0.7 %copy-start.6 = (f32[4,3]{1,0:T(4,128)S(1)}, f32[4,3]{1,0:T(4,128)}, u32[]{:S(2)}) copy-start(f32[4,3]{1,0:T(4,128)} %refs_0_.3) | copy-start | bytes 148

commit v4 on v3

--- a/solution.py
+++ b/solution.py
@@ -142,9 +142,9 @@
 def pre_kernel(
     half_height,
     tiles_view,
-    shift_ref,
-    count_ref,
-    id_ref,
+    shift_hbm,
+    count_hbm,
+    id_hbm,
     centre_hbm,
     scale_hbm,
     rotation_hbm,
@@ -154,10 +154,13 @@
     list_hbm,
     out_ref,
     inverse_ref,
-    view_ref,
+    shifts,
     raw,
     slots,
     marks,
+    shift_ref,
+    count_ref,
+    id_ref,
     centre_ref,
     scale_ref,
     rotation_ref,
@@ -173,12 +176,15 @@
     logit_ref = raw.at[pl.ds(13 * rows, rows), :]
     pairs = [
         (send_hbm, send_ref),
+        (shift_hbm, shift_ref),
         (centre_hbm, centre_ref),
         (scale_hbm, scale_ref),
         (rotation_hbm, rotation_ref),
         (colour_hbm, colour_ref),
         (logit_hbm, logit_ref),
         (list_hbm, list_ref),
+        (count_hbm, count_ref),
+        (id_hbm, id_ref),
     ]
     copies = [
         pltpu.make_async_copy(source, target, arrived.at[i])
@@ -216,8 +222,8 @@
     whole = (total + 0.5).astype(jnp.int32)
     second = whole[rows:]
     inverse_ref[...] = whole[:rows] * 64 + (second & 63)
-    view_ref[...] = second >> 6
-    for copy in copies[1:6]:
+    view = second >> 6
+    for copy in copies[1:7]:
         copy.wait()
     first = 0
     for ref in (centre_ref, scale_ref, rotation_ref, colour_ref):
@@ -225,7 +231,9 @@
         first += ref.shape[0] * rows
     for chunk in range(rows // 8):
         parts = raw_rows(raw, rows, chunk)
-        shift = view_shifts(view_ref[chunk * 8 : chunk * 8 + 8, :], shift_ref)
+        shift = view_shifts(view[chunk * 8 : chunk * 8 + 8, :], shift_ref)
+        for axis in range(3):
+            shifts[axis * rows + chunk * 8 : axis * rows + chunk * 8 + 8, :] = shift[axis]
         for c, value in enumerate(project(parts + (half_height,), shift)):
             table[c * rows + chunk * 8 : c * rows + chunk * 8 + 8, :] = value
     local = [index[i * 8 : i * 8 + 8, :] % owned for i in range(rows // 8)]
@@ -239,7 +247,8 @@
         return carry
 
     lax.fori_loop(0, PARAMS, gather, 0)
-    copies[6].wait()
+    for copy in copies[7:]:
+        copy.wait()
     tiles, length = list_ref.shape
     blocks = length // 128
     lane = iota((8, 128), 1)
@@ -494,10 +503,9 @@
 
 def post_kernel(
     half_height,
-    shift_ref,
     raw,
     inverse_ref,
-    view_ref,
+    shifts,
     table_ref,
     centre_out,
     scale_out,
@@ -521,7 +529,9 @@
     lax.fori_loop(0, PARAMS, gather, 0)
     for chunk in range(rows // 8):
         parts = raw_rows(raw, rows, chunk)
-        shift = view_shifts(view_ref[chunk * 8 : chunk * 8 + 8, :], shift_ref)
+        shift = [
+            shifts[axis * rows + chunk * 8 : axis * rows + chunk * 8 + 8, :] for axis in range(3)
+        ]
         _, pull = jax.vjp(lambda *args: project(args + (half_height,), shift), *parts)
         back = pull([grads[c, chunk * 8 : chunk * 8 + 8, :] for c in range(PARAMS)])
         flat = back[0] + back[1] + back[2] + back[4]
@@ -551,10 +561,8 @@
 
 
 VMEM = pl.BlockSpec(memory_space=pltpu.VMEM)
-SMEM = pl.BlockSpec(memory_space=pltpu.SMEM)
 HBM = pl.BlockSpec(memory_space=pltpu.HBM)
 LIMIT = pltpu.CompilerParams(vmem_limit_bytes=40 * 1024 * 1024)
-FULL = pltpu.CompilerParams(vmem_limit_bytes=60 * 1024 * 1024)
 
 
 def shards(
@@ -583,39 +591,49 @@
     table_shape = jax.ShapeDtypeStruct((rows, 1, ROW), F32)
     whole = jax.ShapeDtypeStruct((rows, 128), jnp.int32)
     entry_shape = jax.ShapeDtypeStruct((tiles * length // 128, 128), jnp.int32)
-    outgoing, inverse, view, raw, slots, marks = pl.pallas_call(
+    outgoing, inverse, shifts, raw, slots, marks = pl.pallas_call(
         lambda *refs: pre_kernel(half_height, tiles_view, *refs),
         out_shape=(
             table_shape,
             whole,
-            whole,
+            jax.ShapeDtypeStruct((3 * rows, 128), F32),
             jax.ShapeDtypeStruct((14 * rows, 128), F32),
             entry_shape,
             entry_shape,
         ),
-        in_specs=[SMEM] * 3 + [HBM] * 7,
+        in_specs=[HBM] * 10,
         out_specs=(VMEM,) * 6,
-        scratch_shapes=[pltpu.VMEM((n, owned), F32) for n in (3, 3, 4, 3)]
+        scratch_shapes=[
+            pltpu.SMEM(view_shift.shape, F32),
+            pltpu.SMEM(tile_counts.shape, jnp.int32),
+            pltpu.SMEM(tile_ids.shape, jnp.int32),
+        ]
+        + [pltpu.VMEM((n, owned), F32) for n in (3, 3, 4, 3)]
         + [
             pltpu.VMEM(targets.shape, jnp.int32),
             pltpu.VMEM(tile_lists.shape, jnp.int32),
             pltpu.VMEM((rows, 128), jnp.int32),
             pltpu.VMEM((PARAMS * rows, 128), F32),
-            pltpu.SemaphoreType.DMA((7,)),
+            pltpu.SemaphoreType.DMA((10,)),
         ],
-        compiler_params=FULL,
+        compiler_params=LIMIT,
         name="project_and_pack",
     )(
-        view_shift,
-        tile_counts,
-        tile_ids,
-        centres,
-        log_scales,
-        rotations,
-        logits,
-        colours,
-        targets,
-        tile_lists,
+        *[
+            pltpu.with_memory_space_constraint(array, pltpu.HBM)
+            for array in (
+                view_shift,
+                tile_counts,
+                tile_ids,
+                centres,
+                log_scales,
+                rotations,
+                logits,
+                colours,
+                targets,
+                tile_lists,
+            )
+        ],
     )
     received = exchange(outgoing, peers, capacity)
     rendered, slot_grads = pl.pallas_call(
@@ -646,7 +664,7 @@
     grads = pl.pallas_call(
         lambda *refs: post_kernel(half_height, *refs),
         out_shape=tuple(shapes),
-        in_specs=[SMEM] + [VMEM] * 4,
+        in_specs=[VMEM] * 4,
         out_specs=(VMEM,) * 5,
         scratch_shapes=[
             pltpu.VMEM((PARAMS, rows, 128), F32),
@@ -654,7 +672,7 @@
         ],
         compiler_params=LIMIT,
         name="unpack_and_project_back",
-    )(view_shift, raw, inverse, view, returned)
+    )(raw, inverse, shifts, returned)
     return (rendered, grads[0], grads[1], grads[2], grads[3].reshape(owned), grads[4])
 
 

time: 49.8 us -> 46.8 us (0.940)
  Pallas kernels: 21.4 us -> 19.6 us
  local copies, waits for them, and re-layouts: 0.71 us -> 0.01 us
    pallas_call x1, Pallas kernels: 5.1 us -> 3.8 us  [shards(): pl.pallas_call(lambda *refs: pre_kernel(half_height, tiles_view, *refs),...]
    unnamed x14 -> x2, local copies, waits for them, and re-layouts: 0.71 us -> 0.01 us
    pallas_call x1, Pallas kernels: 3.52 us -> 2.94 us  [shards(): pl.pallas_call(lambda *refs: post_kernel(half_height, *refs), out_shape=t...]
where the time goes in v4:
time: 46.8 us; the launch traced here: 46.5 us
  blocking collectives  26.3 us (56%)
  Pallas kernels  19.6 us (42%)
  between operations  0.66 us (1%)
    all_to_all x2, blocking collectives, exchange(): return lax.all_to_all(table, PEERS, split_axis=0, concat_axis=0, tiled=True)  26.3 us
    pallas_call x1, Pallas kernels, shards(): pl.pallas_call(lambda *refs: render_kernel(length, *refs), out_shape=(jax...  12.8 us
    pallas_call x1, Pallas kernels, shards(): pl.pallas_call(lambda *refs: pre_kernel(half_height, tiles_view, *refs),...  3.8 us
    pallas_call x1, Pallas kernels, shards(): pl.pallas_call(lambda *refs: post_kernel(half_height, *refs), out_shape=t...  2.94 us

profile of v4, /device:TPU:0, one launch (start us, length us, event | category | flops | bytes accessed | tf_op | source)
XLA Modules:
  0.0 46.5 jit_solution(18166015605662683684)
XLA Ops:
  0.6 3.8 %project_and_pack.1 = (f32[32,1,1152]{2,1,0:T(1,128)S(1)}, s32[32,128]{1,0:T(8,128)S(1)}, f32[96,128]{1,0:T(8,128)S(1)}, f32[448,128]{1,0:T(8,128)S(1)}, s32[64,128]{1,0:T(8,128)S(1)}, /*index=5*/s32[64,128]{1,0:T(8,128)S(1)}) custom-call(f32[4,3]{1,0:T(4,128)} %refs_0_.1, s32[16]{0:T(128)} %refs_1_.1, s32[16]{0:T(128)} %refs_2_.1, f32[3,4096]{1,0:T(4,128)} %refs_3_.2, ...), custom_call_target="tpu_custom_call" | custom-call | tf_op jit(solution)/shard_map/project_and_pack/pallas_call | solution.py:594
  4.4 0.0 copy-start
  4.5 15.5 %all_to_all.10.refs_0_ = f32[32,1,1152]{2,1,0:T(1,128)S(1)} all-to-all(f32[32,1,1152]{2,1,0:T(1,128)S(1)} %get-tuple-element.19), channel_id=1, replica_groups=mesh['groups'=2,'gs'=8,'sub'=2] {'gs','sub'}, dimensions={0} | all-to-all | bytes 294912 | tf_op jit(solution)/shard_map/all_to_all | solution.py:553
  20.0 0.0 copy-done
  20.0 12.8 %render.1 = (f32[3,4096]{1,0:T(4,128)}, f32[32,1,1152]{2,1,0:T(1,128)S(1)}) custom-call(f32[32,1,1152]{2,1,0:T(1,128)S(1)} %all_to_all.10.refs_0_, s32[64,128]{1,0:T(8,128)S(1)} %get-tuple-element.20.refs_1_, s32[64,128]{1,0:T(8,128)S(1)} %get-tuple-element.21.refs_2_, f32[3,4096]{1,0:T(4,128)S(1)} %copy-done), custom_call_target="tpu_custom_call" | custom-call | tf_op jit(solution)/shard_map/render/pallas_call | solution.py:639
  32.8 10.8 %all_to_all.11.refs_3_ = f32[32,1,1152]{2,1,0:T(1,128)S(1)} all-to-all(f32[32,1,1152]{2,1,0:T(1,128)S(1)} %get-tuple-element.26), channel_id=1, replica_groups=mesh['groups'=2,'gs'=8,'sub'=2] {'gs','sub'}, dimensions={0} | all-to-all | bytes 294912 | tf_op jit(solution)/shard_map/all_to_all | solution.py:553
  43.6 2.9 %unpack_and_project_back.1 = (f32[3,4096]{1,0:T(4,128)}, f32[3,4096]{1,0:T(4,128)}, f32[4,4096]{1,0:T(4,128)}, f32[32,128]{1,0:T(8,128)}, f32[3,4096]{1,0:T(4,128)}) custom-call(f32[448,128]{1,0:T(8,128)S(1)} %get-tuple-element.23.refs_0_, s32[32,128]{1,0:T(8,128)S(1)} %get-tuple-element.24.refs_1_, f32[96,128]{1,0:T(8,128)S(1)} %get-tuple-element.25.refs_2_, ...), custom_call_target="tpu_custom_call" | custom-call | tf_op jit(solution)/shard_map/unpack_and_project_back/pallas_call | solution.py:664
Async XLA Ops:
  4.4 15.5 %copy-start = (f32[3,4096]{1,0:T(4,128)S(1)}, f32[3,4096]{1,0:T(4,128)}, u32[]{:S(2)}) copy-start(f32[3,4096]{1,0:T(4,128)} %refs_3_.3) | copy-start | bytes 147460

commit v5 on v4

--- a/solution.py
+++ b/solution.py
@@ -305,8 +305,15 @@
     for k, value in enumerate([py * py, px * py, px, py, jnp.ones_like(px)]):
         features = jnp.where(feature == k + 1, value, features)
     blank = jnp.zeros((24, 256), F32)
-    moment_rows = jnp.concatenate([features, jnp.zeros((8, 256), F32)], 0)
-    moment_rows = jnp.concatenate([moment_rows, moment_rows], 1).astype(BF16)
+    moment = iota((16, 96), 0)
+    power = iota((16, 96), 1) % 48 // 16
+    at = (iota((16, 96), 1) % 16).astype(F32) - 7.5
+    moment_rows = jnp.zeros((16, 96), F32)
+    for k, (y_power, value) in enumerate(
+        [(0, at * at), (2, 1.0), (1, at), (0, at), (1, 1.0), (0, 1.0)]
+    ):
+        moment_rows = jnp.where((moment == k) & (power == y_power), value, moment_rows)
+    moment_rows = moment_rows.astype(BF16)
     run_row = iota((8, 256), 0)
 
     def earlier_product(value):
@@ -359,6 +366,11 @@
             coefs[spread(8 + k), :] = found[6 + k] - BACKGROUND
 
     def chain(g):
+        for i in range(group):
+            summed = dot(moment_rows, buffers[5 * i + 4][...])
+            for b in range(blocks):
+                base = (i * blocks + b) * 16
+                moments[base : base + 8, :] = summed[:8, b * 128 : b * 128 + 128]
         du, dw, a, b, e, o, _ = placed(g, [gathered[g, c] for c in range(6)])
         m_xx, m_yy, m_xy, m_x, m_y, m_one = [moments[spread(k), :] for k in range(6)]
         d_x = m_x - du * m_one
@@ -425,7 +437,7 @@
         tint_rows = jnp.concatenate(tints, 1).astype(BF16)
         return lanes, cot_rows, tint_rows, dot(left, right, TN)
 
-    def render(i, lanes, cot_rows, tint_rows, both, alpha_ref, share_ref, weights, slopes):
+    def render(i, lanes, cot_rows, tint_rows, both, alpha_ref, share_ref, weights, slopes, column_ref):
         left_over = jnp.ones((8, 256), F32)
         for step in range(steps):
             here = slice(step * 16, step * 16 + 16)
@@ -463,19 +475,40 @@
             behind = behind + share[8:]
             first = share[:8] - beta[:8] * behind
             behind = behind + share[:8]
-            high, low = halves(jnp.concatenate([first, second], 0))
-            slopes[here, :256] = high
-            slopes[here, 256:] = low
-        summed = dot(moment_rows, slopes[...], NT)
+            slopes[here, :] = jnp.concatenate([first, second], 0)
+        sums = [[], []]
+        for b in range(blocks):
+            upper, lower = [
+                slopes[b * 128 : b * 128 + 128, side * 128 : side * 128 + 128].T
+                for side in range(2)
+            ]
+            columns = [[], [], []]
+            for x in range(0, 16, 8):
+                parts = [jnp.zeros((8, 128), F32)] * 3
+                for y in range(8):
+                    near = lower[y * 16 + x : y * 16 + x + 8, :]
+                    far = upper[112 - y * 16 + x : 120 - y * 16 + x, :]
+                    both_sides = near + far
+                    parts[0] = parts[0] + both_sides
+                    parts[1] = parts[1] + (y + 0.5) * (near - far)
+                    parts[2] = parts[2] + (y + 0.5) ** 2 * both_sides
+                for k in range(3):
+                    columns[k].append(parts[k])
+            column = jnp.concatenate(columns[0] + columns[1] + columns[2], 0)
+            column_high = column.astype(BF16).astype(F32)
+            sums[0].append(column_high)
+            sums[1].append(column - column_high)
+        summed = jnp.concatenate([jnp.concatenate(part, 1) for part in sums], 0)
+        column_ref[...] = summed.astype(BF16)
         for b in range(blocks):
             base = (i * blocks + b) * 16
-            here = slice(b * 128, b * 128 + 128)
-            moments[base : base + 8, :] = summed[:8, here]
-            moments[base + 8 : base + 16, :] = tint_grad[:, here]
+            moments[base + 8 : base + 16, :] = tint_grad[:, b * 128 : b * 128 + 128]
 
     slot_ref[...] = jnp.zeros(slot_ref.shape, F32)
     moments[...] = jnp.zeros(moments.shape, F32)
     coefs[...] = jnp.zeros(coefs.shape, F32)
+    for i in range(group):
+        buffers[5 * i + 4][...] = jnp.zeros((96, length), BF16)
     gather(0)
 
     def step(g, carry):
@@ -485,7 +518,7 @@
         gather(jnp.minimum(g + 1, groups - 1))
         scatter(before)
         for i in range(group):
-            render(i, *ready[i], *buffers[4 * i : 4 * i + 4])
+            render(i, *ready[i], *buffers[5 * i : 5 * i + 5])
         return carry
 
     lax.fori_loop(0, groups, step, 0)
@@ -652,7 +685,8 @@
             pltpu.VMEM((length, 256), F32),
             pltpu.VMEM((length, 256), F32),
             pltpu.VMEM((length, 512), BF16),
-            pltpu.VMEM((length, 512), BF16),
+            pltpu.VMEM((length, 256), F32),
+            pltpu.VMEM((96, length), BF16),
         ]
         * (1024 // length),
         compiler_params=LIMIT,

time: 46.8 us -> 45.4 us (0.970)
  Pallas kernels: 19.6 us -> 18.1 us
    pallas_call x1, Pallas kernels: 12.8 us -> 11.4 us  [shards(): pl.pallas_call(lambda *refs: render_kernel(length, *refs), out_shape=(jax...]
where the time goes in v5:
time: 45.4 us; the launch traced here: 45.1 us
  blocking collectives  26.3 us (58%)
  Pallas kernels  18.1 us (40%)
  between operations  0.65 us (1%)
    all_to_all x2, blocking collectives, exchange(): return lax.all_to_all(table, PEERS, split_axis=0, concat_axis=0, tiled=True)  26.3 us
    pallas_call x1, Pallas kernels, shards(): pl.pallas_call(lambda *refs: render_kernel(length, *refs), out_shape=(jax...  11.4 us
    pallas_call x1, Pallas kernels, shards(): pl.pallas_call(lambda *refs: pre_kernel(half_height, tiles_view, *refs),...  3.8 us
    pallas_call x1, Pallas kernels, shards(): pl.pallas_call(lambda *refs: post_kernel(half_height, *refs), out_shape=t...  2.94 us

profile of v5, /device:TPU:0, one launch (start us, length us, event | category | flops | bytes accessed | tf_op | source)
XLA Modules:
  0.0 45.1 jit_solution(9116531775596606375)
XLA Ops:
  0.6 3.8 %project_and_pack.1 = (f32[32,1,1152]{2,1,0:T(1,128)S(1)}, s32[32,128]{1,0:T(8,128)S(1)}, f32[96,128]{1,0:T(8,128)S(1)}, f32[448,128]{1,0:T(8,128)S(1)}, s32[64,128]{1,0:T(8,128)S(1)}, /*index=5*/s32[64,128]{1,0:T(8,128)S(1)}) custom-call(f32[4,3]{1,0:T(4,128)} %refs_0_.1, s32[16]{0:T(128)} %refs_1_.1, s32[16]{0:T(128)} %refs_2_.1, f32[3,4096]{1,0:T(4,128)} %refs_3_.2, ...), custom_call_target="tpu_custom_call" | custom-call | tf_op jit(solution)/shard_map/project_and_pack/pallas_call | solution.py:627
  4.4 0.0 copy-start
  4.5 15.5 %all_to_all.10.refs_0_ = f32[32,1,1152]{2,1,0:T(1,128)S(1)} all-to-all(f32[32,1,1152]{2,1,0:T(1,128)S(1)} %get-tuple-element.19), channel_id=1, replica_groups=mesh['groups'=2,'gs'=8,'sub'=2] {'gs','sub'}, dimensions={0} | all-to-all | bytes 294912 | tf_op jit(solution)/shard_map/all_to_all | solution.py:586
  20.0 0.0 copy-done
  20.0 11.4 %render.1 = (f32[3,4096]{1,0:T(4,128)}, f32[32,1,1152]{2,1,0:T(1,128)S(1)}) custom-call(f32[32,1,1152]{2,1,0:T(1,128)S(1)} %all_to_all.10.refs_0_, s32[64,128]{1,0:T(8,128)S(1)} %get-tuple-element.20.refs_1_, s32[64,128]{1,0:T(8,128)S(1)} %get-tuple-element.21.refs_2_, f32[3,4096]{1,0:T(4,128)S(1)} %copy-done), custom_call_target="tpu_custom_call" | custom-call | tf_op jit(solution)/shard_map/render/pallas_call | solution.py:672
  31.4 10.8 %all_to_all.11.refs_3_ = f32[32,1,1152]{2,1,0:T(1,128)S(1)} all-to-all(f32[32,1,1152]{2,1,0:T(1,128)S(1)} %get-tuple-element.26), channel_id=1, replica_groups=mesh['groups'=2,'gs'=8,'sub'=2] {'gs','sub'}, dimensions={0} | all-to-all | bytes 294912 | tf_op jit(solution)/shard_map/all_to_all | solution.py:586
  42.1 2.9 %unpack_and_project_back.1 = (f32[3,4096]{1,0:T(4,128)}, f32[3,4096]{1,0:T(4,128)}, f32[4,4096]{1,0:T(4,128)}, f32[32,128]{1,0:T(8,128)}, f32[3,4096]{1,0:T(4,128)}) custom-call(f32[448,128]{1,0:T(8,128)S(1)} %get-tuple-element.23.refs_0_, s32[32,128]{1,0:T(8,128)S(1)} %get-tuple-element.24.refs_1_, f32[96,128]{1,0:T(8,128)S(1)} %get-tuple-element.25.refs_2_, ...), custom_call_target="tpu_custom_call" | custom-call | tf_op jit(solution)/shard_map/unpack_and_project_back/pallas_call | solution.py:698
Async XLA Ops:
  4.4 15.5 %copy-start = (f32[3,4096]{1,0:T(4,128)S(1)}, f32[3,4096]{1,0:T(4,128)}, u32[]{:S(2)}) copy-start(f32[3,4096]{1,0:T(4,128)} %refs_3_.3) | copy-start | bytes 147460

commit v6 on v5

--- a/solution.py
+++ b/solution.py
@@ -39,15 +39,25 @@
     return high, (value - high.astype(F32)).astype(BF16)
 
 
-def lookup(row_of, index, rows):
+def lookups(row_of, index, rows, channels):
     low = index & 127
     high = index >> 7
-    found = jnp.zeros(index.shape, F32)
+    found = [jnp.zeros(index.shape, F32) for _ in channels]
     for row in range(rows):
-        spread = jnp.broadcast_to(row_of(row), index.shape)
-        taken = jnp.take_along_axis(spread, low, axis=1, mode="promise_in_bounds")
-        found = jnp.where(high == row, taken, found)
+        is_row = high == row
+        for at, c in enumerate(channels):
+            value = jnp.broadcast_to(row_of(c, row), index.shape)
+            value = jnp.take_along_axis(value, low, axis=1, mode="promise_in_bounds")
+            found[at] = jnp.where(is_row, value, found[at])
     return found
+
+
+def shown(logit):
+    return 1.0 / (1.0 + jnp.exp(-logit))
+
+
+def tint(colour):
+    return 0.5 + SH_ZERO * colour
 
 
 def project(raw, shift):
@@ -114,8 +124,8 @@
         screen_yy * inv_det,
         -screen_xy * inv_det,
         screen_xx * inv_det,
-        1.0 / (1.0 + jnp.exp(-logit)),
-    ] + [0.5 + SH_ZERO * part for part in colours]
+        shown(logit),
+    ] + [tint(part) for part in colours]
 
 
 def load_dense(ref, dense, first, rows):
@@ -192,11 +202,36 @@
     ]
     for copy in copies:
         copy.start()
-    copies[0].wait()
+    for copy in copies[:7]:
+        copy.wait()
     per = send_ref.shape[1] // 128
     peers = send_ref.shape[0]
     for part in range(per):
         index[pl.ds(part, peers, stride=per), :] = send_ref[:, part * 128 : part * 128 + 128]
+    first = 0
+    for ref in (centre_ref, scale_ref, rotation_ref, colour_ref):
+        load_dense(ref, raw, first, rows)
+        first += ref.shape[0] * rows
+    for chunk in range(rows // 8):
+        _, _, _, logit, colours = raw_rows(raw, rows, chunk)
+        for c, value in enumerate([shown(logit)] + [tint(part) for part in colours]):
+            at = (5 + c) * rows + chunk * 8
+            table[at : at + 8, :] = value
+
+    def gather(channels):
+        for i in range(rows // 8):
+            local = index[i * 8 : i * 8 + 8, :] % owned
+            found = lookups(
+                lambda c, row: table[c * rows + row : c * rows + row + 1, :],
+                local,
+                rows,
+                channels,
+            )
+            for value, c in zip(found, channels):
+                for s in range(8):
+                    out_ref[i * 8 + s, :, c * 128 : c * 128 + 128] = value[s : s + 1, :]
+
+    gather(range(5, PARAMS))
     total = jnp.zeros((2 * rows, 128), F32)
     group = 8
     for start in range(0, rows, group):
@@ -223,30 +258,14 @@
     second = whole[rows:]
     inverse_ref[...] = whole[:rows] * 64 + (second & 63)
     view = second >> 6
-    for copy in copies[1:7]:
-        copy.wait()
-    first = 0
-    for ref in (centre_ref, scale_ref, rotation_ref, colour_ref):
-        load_dense(ref, raw, first, rows)
-        first += ref.shape[0] * rows
     for chunk in range(rows // 8):
         parts = raw_rows(raw, rows, chunk)
         shift = view_shifts(view[chunk * 8 : chunk * 8 + 8, :], shift_ref)
         for axis in range(3):
             shifts[axis * rows + chunk * 8 : axis * rows + chunk * 8 + 8, :] = shift[axis]
-        for c, value in enumerate(project(parts + (half_height,), shift)):
+        for c, value in enumerate(project(parts + (half_height,), shift)[:5]):
             table[c * rows + chunk * 8 : c * rows + chunk * 8 + 8, :] = value
-    local = [index[i * 8 : i * 8 + 8, :] % owned for i in range(rows // 8)]
-
-    def gather(c, carry):
-        lane = pl.multiple_of(c * 128, 128)
-        for i in range(rows // 8):
-            found = lookup(lambda row: table[pl.ds(c * rows + row, 1), :], local[i], rows)
-            for s in range(8):
-                out_ref[i * 8 + s, :, pl.ds(lane, 128)] = found[s : s + 1, :]
-        return carry
-
-    lax.fori_loop(0, PARAMS, gather, 0)
+    gather(range(5))
     for copy in copies[7:]:
         copy.wait()
     tiles, length = list_ref.shape
@@ -341,15 +360,12 @@
 
     def gather(g):
         index = slots[pl.ds(pl.multiple_of(g * 8, 8), 8), :]
-        low = index & 127
-        high = index >> 7
-        found = [jnp.zeros((8, 128), F32)] * PARAMS
-        for row in range(rows):
-            is_row = high == row
-            for c in range(PARAMS):
-                value = jnp.broadcast_to(table_ref[row, :, c * 128 : c * 128 + 128], (8, 128))
-                value = jnp.take_along_axis(value, low, axis=1, mode="promise_in_bounds")
-                found[c] = jnp.where(is_row, value, found[c])
+        found = lookups(
+            lambda c, row: table_ref[row, :, c * 128 : c * 128 + 128],
+            index,
+            rows,
+            range(PARAMS),
+        )
         for c in range(6):
             gathered[g, c] = found[c]
         du, dw, a, b, e, o, live = placed(g, found[:6])
@@ -391,11 +407,13 @@
     def scatter(g):
         index = slots[pl.ds(pl.multiple_of(g * 8, 8), 8), :]
         lefts, rights = [], []
+        number = iota((256, 128), 0).astype(F32).astype(BF16)
         for r in range(8):
             slot = index[r : r + 1, :]
             match = jnp.broadcast_to(slot >> 8, (rows // 2, 128)) == iota((rows // 2, 128), 0)
-            where = jnp.broadcast_to(slot & 255, (256, 128)) == iota((256, 128), 0)
-            rights.append(jnp.where(where, 1.0, 0.0).astype(BF16))
+            low = (slot & 255).astype(F32).astype(BF16)
+            where = jnp.broadcast_to(low, (256, 128)) == number
+            rights.append(jnp.where(where, jnp.ones((), BF16), jnp.zeros((), BF16)))
             parts = [
                 jnp.where(match, jnp.broadcast_to(grads[c, r : r + 1, :], match.shape), 0.0)
                 for c in range(2 * PARAMS)
@@ -437,7 +455,7 @@
         tint_rows = jnp.concatenate(tints, 1).astype(BF16)
         return lanes, cot_rows, tint_rows, dot(left, right, TN)
 
-    def render(i, lanes, cot_rows, tint_rows, both, alpha_ref, share_ref, weights, slopes, column_ref):
+    def render(i, lanes, cot_rows, tint_rows, both, alpha_ref, weight_ref, weights, slopes, column_ref):
         left_over = jnp.ones((8, 256), F32)
         for step in range(steps):
             here = slice(step * 16, step * 16 + 16)
@@ -458,23 +476,25 @@
             high, low = halves(weight)
             weights[here, :256] = high
             weights[here, 256:] = low
+            weight_ref[here, :] = weight
             share = weight * both[here, 256:]
-            share_ref[here, :] = share
             total = total + (share[:8] + share[8:])
         image = dot(tint_rows, weights[:, :256])
         image_ref[:, lanes] = BACKGROUND + (image[:8] + image[8:])[:3]
         tint_grad = dot(cot_rows, weights[...], NT)
         tint_grad = tint_grad[:8] + tint_grad[8:]
-        behind = later_sum(total)
+        behind = later_sum(total) / through
         for step in reversed(range(steps)):
             here = slice(step * 16, step * 16 + 16)
             alpha = alpha_ref[here, :]
-            share = share_ref[here, :]
-            beta = alpha * (1.0 + alpha * (1.0 + alpha))
-            second = share[8:] - beta[8:] * behind
-            behind = behind + share[8:]
-            first = share[:8] - beta[:8] * behind
-            behind = behind + share[:8]
+            weight = weight_ref[here, :]
+            shade = both[here, 256:]
+            second = shade[8:] - behind
+            behind = behind + alpha[8:] * second
+            first = shade[:8] - behind
+            behind = behind + alpha[:8] * first
+            first = weight[:8] * first
+            second = weight[8:] * second
             slopes[here, :] = jnp.concatenate([first, second], 0)
         sums = [[], []]
         for b in range(blocks):
@@ -545,28 +565,22 @@
     rotation_out,
     logit_out,
     colour_out,
-    grads,
     dense_out,
 ):
     rows = logit_out.shape[0]
-    index = [inverse_ref[i * 8 : i * 8 + 8, :] for i in range(rows // 8)]
-
-    def gather(c, carry):
-        offset = pl.multiple_of(c * 128, 128)
-        for i in range(rows // 8):
-            grads[c, i * 8 : i * 8 + 8, :] = lookup(
-                lambda row: table_ref[row, :, pl.ds(offset, 128)], index[i], rows
-            )
-        return carry
-
-    lax.fori_loop(0, PARAMS, gather, 0)
     for chunk in range(rows // 8):
         parts = raw_rows(raw, rows, chunk)
         shift = [
             shifts[axis * rows + chunk * 8 : axis * rows + chunk * 8 + 8, :] for axis in range(3)
         ]
         _, pull = jax.vjp(lambda *args: project(args + (half_height,), shift), *parts)
-        back = pull([grads[c, chunk * 8 : chunk * 8 + 8, :] for c in range(PARAMS)])
+        found = lookups(
+            lambda c, row: table_ref[row, :, c * 128 : c * 128 + 128],
+            inverse_ref[chunk * 8 : chunk * 8 + 8, :],
+            rows,
+            range(PARAMS),
+        )
+        back = pull(found)
         flat = back[0] + back[1] + back[2] + back[4]
         for k, value in enumerate(flat):
             dense_out[k * rows + chunk * 8 : k * rows + chunk * 8 + 8, :] = value
@@ -700,10 +714,7 @@
         out_shape=tuple(shapes),
         in_specs=[VMEM] * 4,
         out_specs=(VMEM,) * 5,
-        scratch_shapes=[
-            pltpu.VMEM((PARAMS, rows, 128), F32),
-            pltpu.VMEM((13 * rows, 128), F32),
-        ],
+        scratch_shapes=[pltpu.VMEM((13 * rows, 128), F32)],
         compiler_params=LIMIT,
         name="unpack_and_project_back",
     )(raw, inverse, shifts, returned)

time: 45.4 us -> 42.6 us (0.938)
  Pallas kernels: 18.1 us -> 15.4 us
    pallas_call x1, Pallas kernels: 3.8 us -> 2.83 us  [shards(): pl.pallas_call(lambda *refs: pre_kernel(half_height, tiles_view, *refs),...]
    pallas_call x1, Pallas kernels: 11.4 us -> 10.5 us  [shards(): pl.pallas_call(lambda *refs: render_kernel(length, *refs), out_shape=(jax...]
    pallas_call x1, Pallas kernels: 2.94 us -> 2.07 us  [shards(): pl.pallas_call(lambda *refs: post_kernel(half_height, *refs), out_shape=t...]
where the time goes in v6:
time: 42.6 us; the launch traced here: 42.3 us
  blocking collectives  26.3 us (62%)
  Pallas kernels  15.4 us (36%)
  between operations  0.65 us (2%)
    all_to_all x2, blocking collectives, exchange(): return lax.all_to_all(table, PEERS, split_axis=0, concat_axis=0, tiled=True)  26.3 us
    pallas_call x1, Pallas kernels, shards(): pl.pallas_call(lambda *refs: render_kernel(length, *refs), out_shape=(jax...  10.5 us
    pallas_call x1, Pallas kernels, shards(): pl.pallas_call(lambda *refs: pre_kernel(half_height, tiles_view, *refs),...  2.83 us
    pallas_call x1, Pallas kernels, shards(): pl.pallas_call(lambda *refs: post_kernel(half_height, *refs), out_shape=t...  2.07 us

profile of v6, /device:TPU:0, one launch (start us, length us, event | category | flops | bytes accessed | tf_op | source)
XLA Modules:
  0.0 42.3 jit_solution(5549614168222595207)
XLA Ops:
  0.6 2.8 %project_and_pack.1 = (f32[32,1,1152]{2,1,0:T(1,128)S(1)}, s32[32,128]{1,0:T(8,128)S(1)}, f32[96,128]{1,0:T(8,128)S(1)}, f32[448,128]{1,0:T(8,128)S(1)}, s32[64,128]{1,0:T(8,128)S(1)}, /*index=5*/s32[64,128]{1,0:T(8,128)S(1)}) custom-call(f32[4,3]{1,0:T(4,128)} %refs_0_.1, s32[16]{0:T(128)} %refs_1_.1, s32[16]{0:T(128)} %refs_2_.1, f32[3,4096]{1,0:T(4,128)} %refs_3_.2, ...), custom_call_target="tpu_custom_call" | custom-call | tf_op jit(solution)/shard_map/project_and_pack/pallas_call | solution.py:641
  3.5 0.0 copy-start
  3.5 15.5 %all_to_all.10.refs_0_ = f32[32,1,1152]{2,1,0:T(1,128)S(1)} all-to-all(f32[32,1,1152]{2,1,0:T(1,128)S(1)} %get-tuple-element.19), channel_id=1, replica_groups=mesh['groups'=2,'gs'=8,'sub'=2] {'gs','sub'}, dimensions={0} | all-to-all | bytes 294912 | tf_op jit(solution)/shard_map/all_to_all | solution.py:600
  19.0 0.0 copy-done
  19.0 10.5 %render.1 = (f32[3,4096]{1,0:T(4,128)}, f32[32,1,1152]{2,1,0:T(1,128)S(1)}) custom-call(f32[32,1,1152]{2,1,0:T(1,128)S(1)} %all_to_all.10.refs_0_, s32[64,128]{1,0:T(8,128)S(1)} %get-tuple-element.20.refs_1_, s32[64,128]{1,0:T(8,128)S(1)} %get-tuple-element.21.refs_2_, f32[3,4096]{1,0:T(4,128)S(1)} %copy-done), custom_call_target="tpu_custom_call" | custom-call | tf_op jit(solution)/shard_map/render/pallas_call | solution.py:686
  29.5 10.8 %all_to_all.11.refs_3_ = f32[32,1,1152]{2,1,0:T(1,128)S(1)} all-to-all(f32[32,1,1152]{2,1,0:T(1,128)S(1)} %get-tuple-element.26), channel_id=1, replica_groups=mesh['groups'=2,'gs'=8,'sub'=2] {'gs','sub'}, dimensions={0} | all-to-all | bytes 294912 | tf_op jit(solution)/shard_map/all_to_all | solution.py:600
  40.2 2.1 %unpack_and_project_back.1 = (f32[3,4096]{1,0:T(4,128)}, f32[3,4096]{1,0:T(4,128)}, f32[4,4096]{1,0:T(4,128)}, f32[32,128]{1,0:T(8,128)}, f32[3,4096]{1,0:T(4,128)}) custom-call(f32[448,128]{1,0:T(8,128)S(1)} %get-tuple-element.23.refs_0_, s32[32,128]{1,0:T(8,128)S(1)} %get-tuple-element.24.refs_1_, f32[96,128]{1,0:T(8,128)S(1)} %get-tuple-element.25.refs_2_, ...), custom_call_target="tpu_custom_call" | custom-call | tf_op jit(solution)/shard_map/unpack_and_project_back/pallas_call | solution.py:712
Async XLA Ops:
  3.5 15.5 %copy-start = (f32[3,4096]{1,0:T(4,128)S(1)}, f32[3,4096]{1,0:T(4,128)}, u32[]{:S(2)}) copy-start(f32[3,4096]{1,0:T(4,128)} %refs_3_.3) | copy-start | bytes 147460

commit v7 on v6

--- a/solution.py
+++ b/solution.py
@@ -456,46 +456,40 @@
         return lanes, cot_rows, tint_rows, dot(left, right, TN)
 
     def render(i, lanes, cot_rows, tint_rows, both, alpha_ref, weight_ref, weights, slopes, column_ref):
-        left_over = jnp.ones((8, 256), F32)
+        through = jnp.ones((8, 256), F32)
+        total = jnp.zeros((8, 256), F32)
         for step in range(steps):
             here = slice(step * 16, step * 16 + 16)
             alpha = jnp.exp2(both[here, :256])
             alpha_ref[here, :] = alpha
-            keep = 1.0 - alpha
-            left_over = left_over * (keep[:8] * keep[8:])
-        through = earlier_product(left_over)
-        total = jnp.zeros((8, 256), F32)
-        for step in range(steps):
-            here = slice(step * 16, step * 16 + 16)
-            alpha = alpha_ref[here, :]
             first = alpha[:8] * through
             through = through - first
             second = alpha[8:] * through
             through = through - second
             weight = jnp.concatenate([first, second], 0)
+            weight_ref[here, :] = weight
+            share = weight * both[here, 256:]
+            total = total + (share[:8] + share[8:])
+        reach = earlier_product(through)
+        behind = later_sum(total * reach) / (reach * through)
+        for step in reversed(range(steps)):
+            here = slice(step * 16, step * 16 + 16)
+            alpha = alpha_ref[here, :]
+            shade = both[here, 256:]
+            weight = weight_ref[here, :]
+            weight = jnp.concatenate([weight[:8] * reach, weight[8:] * reach], 0)
             high, low = halves(weight)
             weights[here, :256] = high
             weights[here, 256:] = low
-            weight_ref[here, :] = weight
-            share = weight * both[here, 256:]
-            total = total + (share[:8] + share[8:])
+            second = shade[8:] - behind
+            behind = behind + alpha[8:] * second
+            first = shade[:8] - behind
+            behind = behind + alpha[:8] * first
+            slopes[here, :] = jnp.concatenate([weight[:8] * first, weight[8:] * second], 0)
         image = dot(tint_rows, weights[:, :256])
         image_ref[:, lanes] = BACKGROUND + (image[:8] + image[8:])[:3]
         tint_grad = dot(cot_rows, weights[...], NT)
         tint_grad = tint_grad[:8] + tint_grad[8:]
-        behind = later_sum(total) / through
-        for step in reversed(range(steps)):
-            here = slice(step * 16, step * 16 + 16)
-            alpha = alpha_ref[here, :]
-            weight = weight_ref[here, :]
-            shade = both[here, 256:]
-            second = shade[8:] - behind
-            behind = behind + alpha[8:] * second
-            first = shade[:8] - behind
-            behind = behind + alpha[:8] * first
-            first = weight[:8] * first
-            second = weight[8:] * second
-            slopes[here, :] = jnp.concatenate([first, second], 0)
         sums = [[], []]
         for b in range(blocks):
             upper, lower = [

time: 42.6 us -> 42.4 us (level)
  no operation moved by 1% of the time
where the time goes in v7:
time: 42.4 us; the launch traced here: 42.1 us
  blocking collectives  26.3 us (62%)
  Pallas kernels  15.2 us (36%)
  between operations  0.65 us (2%)
    all_to_all x2, blocking collectives, exchange(): return lax.all_to_all(table, PEERS, split_axis=0, concat_axis=0, tiled=True)  26.3 us
    pallas_call x1, Pallas kernels, shards(): pl.pallas_call(lambda *refs: render_kernel(length, *refs), out_shape=(jax...  10.3 us
    pallas_call x1, Pallas kernels, shards(): pl.pallas_call(lambda *refs: pre_kernel(half_height, tiles_view, *refs),...  2.83 us
    pallas_call x1, Pallas kernels, shards(): pl.pallas_call(lambda *refs: post_kernel(half_height, *refs), out_shape=t...  2.07 us

profile of v7, /device:TPU:0, one launch (start us, length us, event | category | flops | bytes accessed | tf_op | source)
XLA Modules:
  0.0 42.1 jit_solution(7300417323238520825)
XLA Ops:
  0.6 2.8 %project_and_pack.1 = (f32[32,1,1152]{2,1,0:T(1,128)S(1)}, s32[32,128]{1,0:T(8,128)S(1)}, f32[96,128]{1,0:T(8,128)S(1)}, f32[448,128]{1,0:T(8,128)S(1)}, s32[64,128]{1,0:T(8,128)S(1)}, /*index=5*/s32[64,128]{1,0:T(8,128)S(1)}) custom-call(f32[4,3]{1,0:T(4,128)} %refs_0_.1, s32[16]{0:T(128)} %refs_1_.1, s32[16]{0:T(128)} %refs_2_.1, f32[3,4096]{1,0:T(4,128)} %refs_3_.2, ...), custom_call_target="tpu_custom_call" | custom-call | tf_op jit(solution)/shard_map/project_and_pack/pallas_call | solution.py:635
  3.5 0.0 copy-start
  3.5 15.5 %all_to_all.10.refs_0_ = f32[32,1,1152]{2,1,0:T(1,128)S(1)} all-to-all(f32[32,1,1152]{2,1,0:T(1,128)S(1)} %get-tuple-element.19), channel_id=1, replica_groups=mesh['groups'=2,'gs'=8,'sub'=2] {'gs','sub'}, dimensions={0} | all-to-all | bytes 294912 | tf_op jit(solution)/shard_map/all_to_all | solution.py:594
  19.0 0.0 copy-done
  19.0 10.3 %render.1 = (f32[3,4096]{1,0:T(4,128)}, f32[32,1,1152]{2,1,0:T(1,128)S(1)}) custom-call(f32[32,1,1152]{2,1,0:T(1,128)S(1)} %all_to_all.10.refs_0_, s32[64,128]{1,0:T(8,128)S(1)} %get-tuple-element.20.refs_1_, s32[64,128]{1,0:T(8,128)S(1)} %get-tuple-element.21.refs_2_, f32[3,4096]{1,0:T(4,128)S(1)} %copy-done), custom_call_target="tpu_custom_call" | custom-call | tf_op jit(solution)/shard_map/render/pallas_call | solution.py:680
  29.3 10.8 %all_to_all.11.refs_3_ = f32[32,1,1152]{2,1,0:T(1,128)S(1)} all-to-all(f32[32,1,1152]{2,1,0:T(1,128)S(1)} %get-tuple-element.26), channel_id=1, replica_groups=mesh['groups'=2,'gs'=8,'sub'=2] {'gs','sub'}, dimensions={0} | all-to-all | bytes 294912 | tf_op jit(solution)/shard_map/all_to_all | solution.py:594
  40.1 2.1 %unpack_and_project_back.1 = (f32[3,4096]{1,0:T(4,128)}, f32[3,4096]{1,0:T(4,128)}, f32[4,4096]{1,0:T(4,128)}, f32[32,128]{1,0:T(8,128)}, f32[3,4096]{1,0:T(4,128)}) custom-call(f32[448,128]{1,0:T(8,128)S(1)} %get-tuple-element.23.refs_0_, s32[32,128]{1,0:T(8,128)S(1)} %get-tuple-element.24.refs_1_, f32[96,128]{1,0:T(8,128)S(1)} %get-tuple-element.25.refs_2_, ...), custom_call_target="tpu_custom_call" | custom-call | tf_op jit(solution)/shard_map/unpack_and_project_back/pallas_call | solution.py:706
Async XLA Ops:
  3.5 15.5 %copy-start = (f32[3,4096]{1,0:T(4,128)S(1)}, f32[3,4096]{1,0:T(4,128)}, u32[]{:S(2)}) copy-start(f32[3,4096]{1,0:T(4,128)} %refs_3_.3) | copy-start | bytes 147460
